TPU v7x, 32 devices: a whole 2x2x4 slice. The times are simulated.
32 devices in a mesh: rep: 8 (over y, x, core), ep: 4 (over z).
Axes of the slice: x: 2, y: 2, z: 4, core: 2. Of those that a mesh axis runs over, the one named last changes fastest.
Arguments:
- tokens: bfloat16 [4096, 2048], P(('rep', 'ep')), may hold values from -6 to 6
- experts: int32 [4096, 2], P(('rep', 'ep')), may hold values from 0 to 3, all different within a row; in each aligned block of 128 rows (0 to 127, 128 to 255, ...) at most 96 rows name the same one
- gates: bfloat16 [4096, 2], P(('rep', 'ep')), may hold values from 0.099609375 to 1
- w_gate: bfloat16 [4, 2048, 1408], P('ep'), may hold values from -0.125 to 0.125
- w_up: bfloat16 [4, 2048, 1408], P('ep'), may hold values from -0.125 to 0.125
- w_down: bfloat16 [4, 1408, 2048], P('ep'), may hold values from -0.15625 to 0.15625
- cotangent: bfloat16 [4096, 2048], P(('rep', 'ep')), may hold values from -1.1953125 to 1.1953125
Outputs:
- layer_out: bfloat16 [4096, 2048], P(('rep', 'ep'))
- input_grads: bfloat16 [4096, 2048], P(('rep', 'ep'))
- gate_grads: bfloat16 [4096, 2], P(('rep', 'ep'))
- grad_gate: float32 [4, 2048, 1408], P('ep', 'rep')
- grad_up: float32 [4, 2048, 1408], P('ep', 'rep')
- grad_down: float32 [4, 1408, 2048], P('ep', 'rep')
Inputs may be any that keep to these rules, and one draw needn't show every extreme that they name: Each row names 2 different experts; the rows of one device name no expert more than 96 times, a bound that some block reaches.
All inputs are finite; a program needn't handle non-finite values.
Results may differ from a plain program's by a relative error of at most 0.013.
Values may be sent and summed in bfloat16 or wider, within the bound.
A program may use at most 128 MiB of HBM per device.

v0:
```python
import jax
import jax.numpy as jnp
from jax import lax
from jax.sharding import PartitionSpec as P


def expert_forward(gate_mat, up_mat, down_mat, rows):
    sources, piece, model_width = rows.shape
    flat_rows = rows.reshape(sources * piece, model_width)
    gate_pre = jnp.dot(flat_rows, gate_mat, preferred_element_type=jnp.float32)
    up_pre = jnp.dot(flat_rows, up_mat, preferred_element_type=jnp.float32)
    activated = gate_pre * jax.nn.sigmoid(gate_pre)
    hidden = (activated * up_pre).astype(jnp.bfloat16)
    expert_out = jnp.dot(hidden, down_mat, preferred_element_type=jnp.float32).astype(jnp.bfloat16)
    ff_width = gate_pre.shape[1]
    return (
        expert_out.reshape(sources, piece, model_width),
        rows,
        gate_pre.reshape(sources, piece, ff_width),
        up_pre.reshape(sources, piece, ff_width),
    )


def expert_backward(out_grads, gate_pre, up_pre, gate_mat, up_mat, down_mat):
    contract = (((1,), (1,)), ((), ()))
    hidden_grad = lax.dot_general(out_grads, down_mat, contract, preferred_element_type=jnp.float32)
    sigmoid_g = jax.nn.sigmoid(gate_pre)
    activated = gate_pre * sigmoid_g
    gate_delta = (hidden_grad * up_pre * sigmoid_g * (1.0 + gate_pre * (1.0 - sigmoid_g))).astype(
        jnp.bfloat16
    )
    up_delta = (hidden_grad * activated).astype(jnp.bfloat16)
    hidden = (activated * up_pre).astype(jnp.bfloat16)
    row_grads = (
        lax.dot_general(gate_delta, gate_mat, contract, preferred_element_type=jnp.float32)
        + lax.dot_general(up_delta, up_mat, contract, preferred_element_type=jnp.float32)
    ).astype(jnp.bfloat16)
    return (gate_delta, up_delta, hidden, row_grads)


def body(tokens, experts, gates, w_gate, w_up, w_down, cotangent):
    tok_rows, model_width = tokens.shape
    top_count = experts.shape[1]
    n_experts = lax.axis_size("ep")
    capacity = 3 * tok_rows * top_count // (2 * n_experts)
    pair_count = tok_rows * top_count
    gate_mat, up_mat, down_mat = (w_gate[0], w_up[0], w_down[0])
    ff_width = gate_mat.shape[1]
    flat_exp = experts.reshape(pair_count)
    onehot = (flat_exp[:, None] == jnp.arange(n_experts, dtype=jnp.int32)[None, :]).astype(
        jnp.int32
    )
    slot_rank = jnp.sum((jnp.cumsum(onehot, axis=0) - onehot) * onehot, axis=1)
    slot_index = flat_exp * capacity + slot_rank
    source = (
        jnp.zeros((n_experts * capacity,), jnp.int32)
        .at[slot_index]
        .set(jnp.arange(pair_count, dtype=jnp.int32))
    )
    filled = jnp.zeros((n_experts * capacity,), jnp.bfloat16).at[slot_index].set(1.0)
    token_src = source // top_count
    dispatch = (tokens[token_src] * filled[:, None]).reshape(n_experts, capacity, model_width)
    expert_out, rows_in, gate_pre, up_pre = expert_forward(
        gate_mat,
        up_mat,
        down_mat,
        lax.all_to_all(dispatch, "ep", split_axis=0, concat_axis=0, tiled=True),
    )
    returned = lax.all_to_all(expert_out, "ep", split_axis=0, concat_axis=0, tiled=True)
    pair_out = returned.reshape(n_experts * capacity, model_width)[slot_index]
    weights = gates.reshape(pair_count, 1).astype(jnp.float32)
    layer_out = jnp.sum(
        (weights * pair_out.astype(jnp.float32)).reshape(tok_rows, top_count, model_width), axis=1
    ).astype(jnp.bfloat16)
    flat_rows = rows_in.reshape(n_experts * capacity, model_width)
    gate_pre = gate_pre.reshape(n_experts * capacity, ff_width)
    up_pre = up_pre.reshape(n_experts * capacity, ff_width)
    gate_grads = jnp.einsum(
        "tkd,td->tk",
        pair_out.reshape(tok_rows, top_count, model_width),
        cotangent,
        preferred_element_type=jnp.float32,
    ).astype(jnp.bfloat16)
    scaled = (weights * jnp.repeat(cotangent, top_count, axis=0).astype(jnp.float32)).astype(
        jnp.bfloat16
    )
    grad_disp = (scaled[source] * filled[:, None]).reshape(n_experts, capacity, model_width)
    out_grads = lax.all_to_all(grad_disp, "ep", split_axis=0, concat_axis=0, tiled=True).reshape(
        n_experts * capacity, model_width
    )
    gate_delta, up_delta, hidden, row_grads = expert_backward(
        out_grads, gate_pre, up_pre, gate_mat, up_mat, down_mat
    )
    back_rows = lax.all_to_all(
        row_grads.reshape(n_experts, capacity, model_width),
        "ep",
        split_axis=0,
        concat_axis=0,
        tiled=True,
    )
    pair_grads = back_rows.reshape(n_experts * capacity, model_width)[slot_index]
    input_grads = jnp.sum(
        pair_grads.astype(jnp.float32).reshape(tok_rows, top_count, model_width), axis=1
    ).astype(jnp.bfloat16)
    rows_first = (((0,), (0,)), ((), ()))
    term_gate = lax.dot_general(
        flat_rows, gate_delta, rows_first, preferred_element_type=jnp.float32
    )
    term_up = lax.dot_general(flat_rows, up_delta, rows_first, preferred_element_type=jnp.float32)
    term_down = lax.dot_general(hidden, out_grads, rows_first, preferred_element_type=jnp.float32)
    grad_gate, grad_up, grad_down = (
        lax.psum_scatter(
            term_gate.astype(jnp.bfloat16), "rep", scatter_dimension=0, tiled=True
        ).astype(jnp.float32),
        lax.psum_scatter(
            term_up.astype(jnp.bfloat16), "rep", scatter_dimension=0, tiled=True
        ).astype(jnp.float32),
        lax.psum_scatter(
            term_down.astype(jnp.bfloat16), "rep", scatter_dimension=0, tiled=True
        ).astype(jnp.float32),
    )
    return (layer_out, input_grads, gate_grads, grad_gate[None], grad_up[None], grad_down[None])


def solution(mesh):
    in_specs = (
        P(("rep", "ep"), None),
        P(("rep", "ep"), None),
        P(("rep", "ep"), None),
        P("ep", None, None),
        P("ep", None, None),
        P("ep", None, None),
        P(("rep", "ep"), None),
    )
    out_specs = (
        P(("rep", "ep"), None),
        P(("rep", "ep"), None),
        P(("rep", "ep"), None),
        P("ep", "rep", None),
        P("ep", "rep", None),
        P("ep", "rep", None),
    )
    return jax.shard_map(body, mesh=mesh, in_specs=in_specs, out_specs=out_specs, check_vma=False)
```

profile of v0, /device:TPU:0, one launch (start us, length us, event | category | flops | bytes accessed | tf_op | source)
XLA Modules:
  0.0 323.4 jit_solution(12454307254198588047)
XLA Ops:
  7.2 0.0 copy-start
  7.2 0.7 broadcast_multiply_fusion.2
  7.9 0.8 copy.18
  8.7 0.1 eq.29
  8.8 0.1 eq.25
  9.0 0.1 copy.17
  9.1 0.1 mul.80
  9.2 0.8 copy.16
  10.0 0.1 reshape.120
  10.2 1.2 reduce-window.6
  11.4 0.1 slice.16
  11.5 0.1 copy.20
  11.6 0.1 copy.21
  11.7 0.1 add_bitcast_fusion
  11.8 2.2 scatter_custom_fusion.1
  14.0 0.1 mul.82
  14.1 1.4 scatter_custom_fusion
  15.5 2.1 broadcast_in_dim.43
  17.6 2.5 convert_element_type.82
  20.1 3.1 gather_fusion
  23.2 0.2 multiply_convert_fusion.3
  23.4 3.1 gather_fusion.2
  26.5 0.0 copy-done.3
  26.5 2.8 broadcast_multiply_fusion
  29.4 43.1 %all_to_all.20 = bf16[4,96,2048]{2,1,0:T(8,128)(2,1)S(1)} all-to-all(bf16[4,96,2048]{2,1,0:T(8,128)(2,1)S(1)} %get-tuple-element.12), channel_id=1, replica_groups=mesh['rep'=8,'ep'=4] {'ep'}, dimensions={0} | all-to-all | bytes 3145728 | tf_op jit(solution)/shard_map/all_to_all | solution.py:67
  72.4 3.6 %all-to-all-start.2 = ((bf16[4,96,2048]{2,1,0:T(8,128)(2,1)}), bf16[4,96,2048]{2,1,0:T(8,128)(2,1)S(1)}, u32[]{:S(2)}, u32[]{:S(2)}) async-start(bf16[4,96,2048]{2,1,0:T(8,128)(2,1)} %get-tuple-element.11), calls=%async_computation.2 | async-start | bytes 3145728 | tf_op jit(solution)/shard_map/all_to_all | solution.py:88
  76.0 0.2 reduce-scatter.8.cloned.1.call-start
  76.2 6.6 %fusion.6 = f32[384,1408]{1,0:T(8,128)} fusion(bf16[384,2048]{1,0:T(8,128)(2,1)S(1)} %bitcast.82, bf16[1,2048,1408]{2,1,0:T(8,128)(2,1)} %param.11), kind=kOutput, calls=%fused_computation.15 | convolution fusion | flops 2214592512 | bytes 9502720 | tf_op jit(solution)/shard_map/dot_general | solution.py:11
  82.8 29.2 %all-to-all-done.2 = bf16[4,96,2048]{2,1,0:T(8,128)(2,1)S(1)} async-done(((bf16[4,96,2048]{2,1,0:T(8,128)(2,1)}), bf16[4,96,2048]{2,1,0:T(8,128)(2,1)S(1)}, u32[]{:S(2)}, u32[]{:S(2)}) %all-to-all-start.2) | async-done | bytes 1572896 | tf_op jit(solution)/shard_map/all_to_all | solution.py:88
  112.1 5.4 %fusion = f32[384,1408]{1,0:T(8,128)S(1)} fusion(bf16[384,2048]{1,0:T(8,128)(2,1)S(1)} %bitcast.87, bf16[1,1408,2048]{2,1,0:T(8,128)(2,1)} %param.12), kind=kOutput, calls=%fused_computation.9 | convolution fusion | flops 2214592512 | bytes 9502720 | tf_op jit(solution)/shard_map/dot_general | solution.py:26
  117.5 7.2 %multiply_convert_fusion.1 = (bf16[384,1408]{1,0:T(8,128)(2,1)}, bf16[384,1408]{1,0:T(8,128)(2,1)}, bf16[384,1408]{1,0:T(8,128)(2,1)S(1)}) fusion(f32[384,1408]{1,0:T(8,128)S(1)} %fusion, f32[384,1408]{1,0:T(8,128)S(1)} %copy-done.10, bf16[384,2048]{1,0:T(8,128)(2,1)S(1)} %bitcast.83, bf16[1,2048,1408]{2,1,0:T(8,128)(2,1)} %param.10), kind=kOutput, calls=%fused_computation.24 | convolution fusion | flops 2222702592 | bytes 14909440 | tf_op jit(solution)/shard_map/dot_general | solution.py:10
  124.8 1.0 copy-done.7
  125.7 5.0 %convolution_convert_fusion = bf16[1408,2048]{1,0:T(8,128)(2,1)} fusion(bf16[384,1408]{1,0:T(8,128)(2,1)S(1)} %get-tuple-element.8, bf16[384,2048]{1,0:T(8,128)(2,1)S(1)} %bitcast.88), kind=kOutput, calls=%fused_computation.6 | convolution fusion | flops 2217476096 | bytes 8421376 | tf_op jit(solution)/shard_map/dot_general | solution.py:110
  130.8 0.0 reduce-scatter.8.cloned.1.call-update
  130.8 0.0 reduce-scatter.4.cloned.1.call-start
  130.9 1.2 copy-done.9
  132.0 5.2 %convolution_convert_fusion.2 = bf16[2048,1408]{1,0:T(8,128)(2,1)} fusion(bf16[384,2048]{1,0:T(8,128)(2,1)S(1)} %bitcast.84, bf16[384,1408]{1,0:T(8,128)(2,1)S(1)} %copy-done.9), kind=kOutput, calls=%fused_computation.8 | convolution fusion | flops 2217476096 | bytes 8421376 | tf_op jit(solution)/shard_map/dot_general | solution.py:106
  137.2 0.0 reduce-scatter.4.cloned.1.call-update
  137.3 0.0 reduce-scatter.6.cloned.1.call-start
  137.3 6.7 %convolution_convert_fusion.1 = bf16[2048,1408]{1,0:T(8,128)(2,1)} fusion(bf16[384,2048]{1,0:T(8,128)(2,1)S(1)} %bitcast.85, bf16[384,1408]{1,0:T(8,128)(2,1)} %get-tuple-element.7), kind=kOutput, calls=%fused_computation.7 | convolution fusion | flops 2217476096 | bytes 8421376 | tf_op jit(solution)/shard_map/dot_general | solution.py:109
  144.0 0.0 reduce-scatter.6.cloned.1.call-update
  144.0 1.2 copy-done.8
  145.3 6.4 %fusion.14 = bf16[384,2048]{1,0:T(8,128)(2,1)} fusion(bf16[384,1408]{1,0:T(8,128)(2,1)S(1)} %copy-done.8, bf16[1,1408,2048]{2,1,0:T(8,128)(2,1)} %param.12), kind=kOutput, calls=%fused_computation.22 | convolution fusion | flops 2215378944 | bytes 8421376 | tf_op jit(solution)/shard_map/dot_general | solution.py:14
  151.7 3.8 %all-to-all-start.1 = ((bf16[4,96,2048]{2,1,0:T(8,128)(2,1)}), bf16[4,96,2048]{2,1,0:T(8,128)(2,1)S(1)}, u32[]{:S(2)}, u32[]{:S(2)}) async-start(bf16[4,96,2048]{2,1,0:T(8,128)(2,1)} %bitcast.9), calls=%async_computation.1 | async-start | bytes 3145728 | tf_op jit(solution)/shard_map/all_to_all | solution.py:69
  155.5 5.0 %fusion.4 = f32[384,2048]{1,0:T(8,128)S(1)} fusion(bf16[384,1408]{1,0:T(8,128)(2,1)} %get-tuple-element.7, bf16[1,2048,1408]{2,1,0:T(8,128)(2,1)} %param.11), kind=kOutput, calls=%fused_computation.13 | convolution fusion | flops 2214592512 | bytes 9994240 | tf_op jit(solution)/shard_map/dot_general | solution.py:36
  160.5 7.8 %add_convert_fusion = bf16[384,2048]{1,0:T(8,128)(2,1)} fusion(f32[384,2048]{1,0:T(8,128)S(1)} %fusion.4, bf16[384,1408]{1,0:T(8,128)(2,1)S(1)} %copy-done.9, bf16[1,2048,1408]{2,1,0:T(8,128)(2,1)} %param.10), kind=kOutput, calls=%fused_computation.21 | convolution fusion | flops 2216165376 | bytes 11567104 | tf_op jit(solution)/shard_map/dot_general | solution.py:35
  168.3 23.5 %all-to-all-done.1 = bf16[4,96,2048]{2,1,0:T(8,128)(2,1)S(1)} async-done(((bf16[4,96,2048]{2,1,0:T(8,128)(2,1)}), bf16[4,96,2048]{2,1,0:T(8,128)(2,1)S(1)}, u32[]{:S(2)}, u32[]{:S(2)}) %all-to-all-start.1) | async-done | bytes 1572896 | tf_op jit(solution)/shard_map/all_to_all | solution.py:69
  191.8 3.6 %all-to-all-start.3 = ((bf16[4,96,2048]{2,1,0:T(8,128)(2,1)}), bf16[4,96,2048]{2,1,0:T(8,128)(2,1)S(1)}, u32[]{:S(2)}, u32[]{:S(2)}) async-start(bf16[4,96,2048]{2,1,0:T(8,128)(2,1)} %bitcast.86), calls=%async_computation.3 | async-start | bytes 3145728 | tf_op jit(solution)/shard_map/all_to_all | solution.py:94
  195.4 2.3 gather_fusion.1
  197.7 2.0 gather.23
  199.7 0.0 copy-start.4
  199.7 2.3 fusion.18
  202.0 0.6 copy.24
  202.6 29.1 %all-to-all-done.3 = bf16[4,96,2048]{2,1,0:T(8,128)(2,1)S(1)} async-done(((bf16[4,96,2048]{2,1,0:T(8,128)(2,1)}), bf16[4,96,2048]{2,1,0:T(8,128)(2,1)S(1)}, u32[]{:S(2)}, u32[]{:S(2)}) %all-to-all-start.3) | async-done | bytes 1572896 | tf_op jit(solution)/shard_map/all_to_all | solution.py:94
  231.8 1.4 gather_fusion.3
  233.1 0.0 copy-start.5
  233.1 0.7 gather.27
  233.9 3.6 %reduce_sum.35 = bf16[128,2048]{1,0:T(8,128)(2,1)} reduce(bf16[128,2,2048]{2,1,0:T(2,128)(2,1)S(1)} %gather.27, bf16[]{:T(256)} %constant.33.clone.1), dimensions={1}, to_apply=%region_6.7 | reduce | flops 262144 | bytes 1572866 | tf_op jit(solution)/shard_map/reduce_sum | solution.py:102
  237.5 3.9 %multiply_reduce_fusion = bf16[128,2048]{1,0:T(8,128)(2,1)} fusion(bf16[128,2,2048]{2,1,0:T(2,128)(2,1)S(1)} %copy-done.5, f32[128,2]{1,0:T(8,128)S(1)} %copy.16), kind=kLoop, calls=%fused_computation.29 | loop fusion | flops 1310720 | bytes 1573888 | tf_op jit(solution)/shard_map/reduce_sum | solution.py:72
  241.4 2.4 bitcast_convert_fusion
  243.7 8.3 %reduce-scatter.4.cloned.1.call-done = bf16[256,1408]{1,0:T(8,128)(2,1)} async-done(((bf16[2048,1408]{1,0:T(8,128)(2,1)}), bf16[256,1408]{1,0:T(8,128)(2,1)}) %reduce-scatter.4.cloned.1.call-update) | async-done | bytes 720912 | tf_op jit(solution)/shard_map/reduce_scatter | solution.py:112
  252.0 2.4 bitcast_convert_fusion.2
  254.4 60.2 %reduce-scatter.6.cloned.1.call-done = bf16[256,1408]{1,0:T(8,128)(2,1)} async-done(((bf16[2048,1408]{1,0:T(8,128)(2,1)}), bf16[256,1408]{1,0:T(8,128)(2,1)}) %reduce-scatter.6.cloned.1.call-update) | async-done | bytes 720912 | tf_op jit(solution)/shard_map/reduce_scatter | solution.py:115
  314.6 2.3 bitcast_convert_fusion.1
  (26 shorter events, 0.1 us)
Async XLA Ops:
  7.2 12.9 %copy-start = (bf16[128,2048]{1,0:T(8,128)(2,1)S(1)}, bf16[128,2048]{1,0:T(8,128)(2,1)}, u32[]{:S(2)}) copy-start(bf16[128,2048]{1,0:T(8,128)(2,1)} %param.7) | copy-start | bytes 1572868
  20.1 3.1 copy-start.2
  23.4 3.1 copy-start.3
  72.4 39.6 %all-to-all-start.2 = ((bf16[4,96,2048]{2,1,0:T(8,128)(2,1)}), bf16[4,96,2048]{2,1,0:T(8,128)(2,1)S(1)}, u32[]{:S(2)}, u32[]{:S(2)}) async-start(bf16[4,96,2048]{2,1,0:T(8,128)(2,1)} %get-tuple-element.11), calls=%async_computation.2 | async-start | bytes 3145728 | tf_op jit(solution)/shard_map/all_to_all | solution.py:88
  76.0 165.4 %reduce-scatter.8.cloned.1.call-start = ((), (), s32[]{:S(2)}) async-start(), calls=%async_computation.9 | async-start | bytes 6488064 | tf_op jit(solution)/shard_map/reduce_scatter | solution.py:118
  112.1 5.4 %copy-start.10 = (f32[384,1408]{1,0:T(8,128)S(1)}, f32[384,1408]{1,0:T(8,128)}, u32[]{:S(2)}) copy-start(f32[384,1408]{1,0:T(8,128)} %fusion.6) | copy-start | bytes 6488068
  124.8 1.0 copy-start.7
  130.8 1.2 copy-start.9
  130.8 121.2 %reduce-scatter.4.cloned.1.call-start = ((), (), s32[]{:S(2)}) async-start(), calls=%async_computation.7 | async-start | bytes 6488064 | tf_op jit(solution)/shard_map/reduce_scatter | solution.py:112
  137.3 177.3 %reduce-scatter.6.cloned.1.call-start = ((), (), s32[]{:S(2)}) async-start(), calls=%async_computation.8 | async-start | bytes 6488064 | tf_op jit(solution)/shard_map/reduce_scatter | solution.py:115
  144.0 1.3 copy-start.8
  151.7 40.1 %all-to-all-start.1 = ((bf16[4,96,2048]{2,1,0:T(8,128)(2,1)}), bf16[4,96,2048]{2,1,0:T(8,128)(2,1)S(1)}, u32[]{:S(2)}, u32[]{:S(2)}) async-start(bf16[4,96,2048]{2,1,0:T(8,128)(2,1)} %bitcast.9), calls=%async_computation.1 | async-start | bytes 3145728 | tf_op jit(solution)/shard_map/all_to_all | solution.py:69
  191.8 40.0 %all-to-all-start.3 = ((bf16[4,96,2048]{2,1,0:T(8,128)(2,1)}), bf16[4,96,2048]{2,1,0:T(8,128)(2,1)S(1)}, u32[]{:S(2)}, u32[]{:S(2)}) async-start(bf16[4,96,2048]{2,1,0:T(8,128)(2,1)} %bitcast.86), calls=%async_computation.3 | async-start | bytes 3145728 | tf_op jit(solution)/shard_map/all_to_all | solution.py:94
  197.7 2.0 copy-start.6
  199.7 2.3 copy-start.4
  233.1 4.4 %copy-start.5 = (bf16[128,2,2048]{2,1,0:T(2,128)(2,1)S(1)}, bf16[128,2,2048]{2,1,0:T(2,128)(2,1)}, u32[]{:S(2)}) copy-start(bf16[128,2,2048]{2,1,0:T(2,128)(2,1)} %copy-done.4) | copy-start | bytes 3145732
  252.0 64.8 %copy-start.1 = (bf16[128,2048]{1,0:T(8,128)(2,1)S(1)}, bf16[128,2048]{1,0:T(8,128)(2,1)}, u32[]{:S(2)}) copy-start(bf16[128,2048]{1,0:T(8,128)(2,1)} %param.7) | copy-start | bytes 1572868
Sparse Core Ops, SparseCore 0:
  130.9 58.1 reduce-scatter.7
  193.0 59.0 reduce-scatter.3
  255.5 59.0 reduce-scatter.5
where the time goes:
time: 324 us; the launch traced here: 323 us
  waiting for transfers between devices  150 us (46%)
  matrix products  57.7 us (18%)
  blocking collectives  43.1 us (13%)
  local copies, waits for them, and re-layouts  27.4 us (8%)
  other arithmetic  19.7 us (6%)
  between operations  14 us (4%)
  starting transfers between devices  11.3 us (3%)
    reduce_scatter x1, waiting for transfers between devices, body(): lax.psum_scatter(term_up.astype(jnp.bfloat16), 'rep', scatter_dimension=0...  60.2 us
    all_to_all x1, blocking collectives, body(): lax.all_to_all(dispatch, 'ep', split_axis=0, concat_axis=0, tiled=True)  43.1 us
    all_to_all x1, waiting for transfers between devices, body(): lax.all_to_all(grad_disp, 'ep', split_axis=0, concat_axis=0, tiled=True)  29.2 us
    all_to_all x1, waiting for transfers between devices, body(): lax.all_to_all(row_grads.reshape(n_experts, capacity, model_width), 'ep',...  29.1 us
    all_to_all x1, waiting for transfers between devices, body(): lax.all_to_all(expert_out, 'ep', split_axis=0, concat_axis=0, tiled=True)  23.5 us
    reduce_scatter x1, waiting for transfers between devices, body(): lax.psum_scatter(term_gate.astype(jnp.bfloat16), 'rep', scatter_dimension...  8.3 us
    dot_general x1, matrix products, expert_backward(): lax.dot_general(gate_delta, gate_mat, contract, preferred_element_type=jn...  7.77 us
    dot_general x1, matrix products, expert_forward(): gate_pre = jnp.dot(flat_rows, gate_mat, preferred_element_type=jnp.float32)  7.25 us
  transfers between devices with their start and end apart: 6, of which 5 were waited for; matrix products, arithmetic and copies ran while one was open for 18% of the time, Pallas kernels for 0%

commit v1 on v0

v1 whole, which is shorter than its diff:
```python
import jax
import jax.numpy as jnp
from jax import lax
from jax.sharding import PartitionSpec as P

F32 = jnp.float32
BF16 = jnp.bfloat16


def dot(lhs, rhs, lhs_dim, rhs_dim):
    contract = (((lhs_dim,), (rhs_dim,)), ((), ()))
    return lax.dot_general(lhs, rhs, contract, preferred_element_type=F32)


def exchange(rows):
    return lax.all_to_all(rows, "ep", split_axis=0, concat_axis=0, tiled=True)


def after(value, *others):
    return lax.optimization_barrier((value, *others))[0]


def body(tokens, experts, gates, w_gate, w_up, w_down, cotangent):
    tok_rows, width = tokens.shape
    top_count = experts.shape[1]
    n_experts = lax.axis_size("ep")
    capacity = 3 * tok_rows * top_count // (2 * n_experts)
    slots = n_experts * capacity
    gate_mat, up_mat, down_mat = (w_gate[0], w_up[0], w_down[0])

    ids = jnp.arange(n_experts, dtype=jnp.int32)
    named = (experts[:, :, None] == ids).astype(BF16)
    visits = jnp.sum(named, axis=1)
    rows = jnp.arange(tok_rows, dtype=jnp.int32)
    earlier = (rows[:, None] > rows[None, :]).astype(BF16)
    rank = dot(earlier, visits, 1, 0)
    place = rank + (ids * capacity).astype(F32)[None, :]
    slot = jnp.sum(named.astype(F32) * place[:, None, :], axis=2).astype(jnp.int32)
    hit = [
        slot[:, k][:, None] == jnp.arange(slots, dtype=jnp.int32)[None, :]
        for k in range(top_count)
    ]
    picks = [h.astype(BF16) for h in hit]
    pick = sum(picks[1:], picks[0])
    weights = gates.astype(F32)

    dispatch = dot(pick, tokens, 0, 0).astype(BF16)
    rows_in = exchange(dispatch.reshape(n_experts, capacity, width)).reshape(slots, width)

    slot_gate = sum(
        jnp.sum(h.astype(F32) * weights[:, k][:, None], axis=0) for k, h in enumerate(hit)
    )
    grad_disp = (dot(pick, cotangent, 0, 0) * slot_gate[:, None]).astype(BF16)
    out_grads = exchange(
        after(grad_disp, rows_in).reshape(n_experts, capacity, width)
    ).reshape(slots, width)

    gate_pre = dot(rows_in, gate_mat, 1, 0)
    up_pre = dot(rows_in, up_mat, 1, 0)
    sigmoid_g = jax.nn.sigmoid(gate_pre)
    activated = gate_pre * sigmoid_g
    hidden = (activated * up_pre).astype(BF16)
    expert_out = dot(hidden, down_mat, 1, 0).astype(BF16)
    returned = exchange(
        after(expert_out, out_grads).reshape(n_experts, capacity, width)
    ).reshape(slots, width)

    def summed(term):
        return lax.psum_scatter(term.astype(BF16), "rep", scatter_dimension=0, tiled=True)

    grad_down = summed(dot(hidden, out_grads, 0, 0))

    hidden_grad = dot(out_grads, down_mat, 1, 1)
    gate_delta = (
        hidden_grad * up_pre * sigmoid_g * (1.0 + gate_pre * (1.0 - sigmoid_g))
    ).astype(BF16)
    up_delta = (hidden_grad * activated).astype(BF16)
    grad_gate = summed(dot(rows_in, gate_delta, 0, 0))
    grad_up = summed(dot(rows_in, up_delta, 0, 0))
    row_grads = (dot(gate_delta, gate_mat, 1, 1) + dot(up_delta, up_mat, 1, 1)).astype(BF16)
    back_rows = exchange(row_grads.reshape(n_experts, capacity, width)).reshape(slots, width)

    layer_out = 0.0
    dots = []
    for k in range(top_count):
        pair_out = dot(picks[k], returned, 1, 0)
        layer_out = layer_out + weights[:, k][:, None] * pair_out
        dots.append(jnp.sum(pair_out * cotangent.astype(F32), axis=1))
    gate_grads = jnp.stack(dots, axis=1).astype(BF16)
    input_grads = dot(pick, back_rows, 1, 0).astype(BF16)
    return (
        layer_out.astype(BF16),
        input_grads,
        gate_grads,
        grad_gate.astype(F32)[None],
        grad_up.astype(F32)[None],
        grad_down.astype(F32)[None],
    )


def solution(mesh):
    tok = P(("rep", "ep"), None)
    mat = P("ep", None, None)
    grad = P("ep", "rep", None)
    return jax.shard_map(
        body,
        mesh=mesh,
        in_specs=(tok, tok, tok, mat, mat, mat, tok),
        out_specs=(tok, tok, tok, grad, grad, grad),
        check_vma=False,
    )
```

time: 324 us -> 308 us (0.951)
  waiting for transfers between devices: 150 us -> 199 us
  blocking collectives: 43.1 us -> 0 us
  local copies, waits for them, and re-layouts: 27.4 us -> 1.57 us
  other arithmetic: 19.7 us -> 9.21 us
  matrix products: 57.7 us -> 64.7 us
  starting transfers between devices: 11.3 us -> 18.3 us
    all_to_all x1 -> x0, blocking collectives: 43.1 us -> none  [body(): lax.all_to_all(dispatch, 'ep', split_axis=0, concat_axis=0, tiled=True)]
    all_to_all x3 -> x4, waiting for transfers between devices: 81.9 us -> 122 us  [exchange(): return lax.all_to_all(rows, 'ep', split_axis=0, concat_axis=0, tiled=True)]
    gather x6 -> x0, local copies, waits for them, and re-layouts: 12.6 us -> none  [the longest x2 4.28 us: body(): pair_out = returned.reshape(n_experts * capacity, model_width)[slot_index]]
    reduce_scatter x3, waiting for transfers between devices: 68.5 us -> 77 us  [summed(): lax.psum_scatter(term.astype(BF16), 'rep', scatter_dimension=0, tiled=True)]
    all_to_all x3 -> x4, starting transfers between devices: 11 us -> 18 us  [exchange(): return lax.all_to_all(rows, 'ep', split_axis=0, concat_axis=0, tiled=True)]
    dot_general x10 -> x15, matrix products: 57.7 us -> 64.7 us  [dot(): return lax.dot_general(lhs, rhs, contract, preferred_element_type=F32)]
    reduce_sum x3, other arithmetic: 7.52 us -> 1.64 us  [the longest x1 0.75 us: body(): visits = jnp.sum(named, axis=1)]
    mul x2 -> x0, other arithmetic: 3.57 us -> none  [the longest x1 2.83 us: body(): scaled[source] * filled[:, None]]
  transfers between devices with their start and end apart: 6 -> 7, of which waited for: 5 -> 6; matrix products, arithmetic and copies ran while one was open for 18% -> 16% of each run, Pallas kernels for 0% -> 0%
where the time goes in v1:
time: 308 us; the launch traced here: 307 us
  waiting for transfers between devices  199 us (65%)
  matrix products  64.7 us (21%)
  starting transfers between devices  18.3 us (6%)
  between operations  13.9 us (5%)
  other arithmetic  9.21 us (3%)
    all_to_all x4, waiting for transfers between devices, exchange(): return lax.all_to_all(rows, 'ep', split_axis=0, concat_axis=0, tiled=True)  122 us
    reduce_scatter x3, waiting for transfers between devices, summed(): lax.psum_scatter(term.astype(BF16), 'rep', scatter_dimension=0, tiled=True)  77 us
    dot_general x15, matrix products, dot(): return lax.dot_general(lhs, rhs, contract, preferred_element_type=F32)  64.7 us
    all_to_all x4, starting transfers between devices, exchange(): return lax.all_to_all(rows, 'ep', split_axis=0, concat_axis=0, tiled=True)  18 us
  transfers between devices with their start and end apart: 7, of which 6 were waited for; matrix products, arithmetic and copies ran while one was open for 16% of the time, Pallas kernels for 0%

profile of v1, /device:TPU:0, one launch (start us, length us, event | category | flops | bytes accessed | tf_op | source)
XLA Modules:
  0.0 306.7 jit_solution(16025951110430455094)
XLA Ops:
  7.2 0.0 copy-start
  7.2 0.7 fusion.37
  7.9 0.1 convolution_add_fusion
  8.1 0.7 multiply_reduce_fusion
  8.8 0.0 copy-done
  8.8 1.8 convolution_convert_fusion.3
  10.7 0.0 copy-start.4
  10.7 0.0 copy-start.2
  10.7 6.4 %all-to-all-start = ((bf16[4,96,2048]{2,1,0:T(8,128)(2,1)}), bf16[4,96,2048]{2,1,0:T(8,128)(2,1)S(1)}, u32[]{:S(2)}, u32[]{:S(2)}) async-start(bf16[4,96,2048]{2,1,0:T(8,128)(2,1)} %bitcast.3), calls=%async_computation | async-start | bytes 3145728 | tf_op jit(solution)/shard_map/all_to_all | solution.py:16
  17.1 0.0 copy-done.4
  17.1 0.1 select_reduce_fusion
  17.3 0.0 copy-done.2
  17.3 1.8 multiply_convert_fusion
  19.1 34.9 %all-to-all-done = bf16[4,96,2048]{2,1,0:T(8,128)(2,1)S(1)} async-done(((bf16[4,96,2048]{2,1,0:T(8,128)(2,1)}), bf16[4,96,2048]{2,1,0:T(8,128)(2,1)S(1)}, u32[]{:S(2)}, u32[]{:S(2)}) %all-to-all-start) | async-done | bytes 1572896 | tf_op jit(solution)/shard_map/all_to_all | solution.py:16
  54.1 4.3 %all-to-all-start.1 = ((bf16[4,96,2048]{2,1,0:T(8,128)(2,1)}), bf16[4,96,2048]{2,1,0:T(8,128)(2,1)}, u32[]{:S(2)}, u32[]{:S(2)}) async-start(bf16[4,96,2048]{2,1,0:T(8,128)(2,1)} %bitcast.9), calls=%async_computation.1 | async-start | bytes 3145728 | tf_op jit(solution)/shard_map/all_to_all | solution.py:16
  58.4 0.0 reduce-scatter.4.cloned.1.call-start
  58.5 6.6 %fusion.6 = f32[384,1408]{1,0:T(8,128)} fusion(bf16[384,2048]{1,0:T(8,128)(2,1)S(1)} %bitcast.73, bf16[1,2048,1408]{2,1,0:T(8,128)(2,1)} %param.11), kind=kOutput, calls=%fused_computation.9 | convolution fusion | flops 2214592512 | bytes 9502720 | tf_op jit(solution)/shard_map/dot_general | solution.py:12
  65.1 29.9 %all-to-all-done.1 = bf16[4,96,2048]{2,1,0:T(8,128)(2,1)} async-done(((bf16[4,96,2048]{2,1,0:T(8,128)(2,1)}), bf16[4,96,2048]{2,1,0:T(8,128)(2,1)}, u32[]{:S(2)}, u32[]{:S(2)}) %all-to-all-start.1) | async-done | bytes 1572896 | tf_op jit(solution)/shard_map/all_to_all | solution.py:16
  95.0 0.0 copy-start.7
  95.0 5.9 %fusion = f32[384,1408]{1,0:T(8,128)S(1)} fusion(bf16[384,2048]{1,0:T(8,128)(2,1)} %bitcast.10, bf16[1,1408,2048]{2,1,0:T(8,128)(2,1)} %param.12), kind=kOutput, calls=%fused_computation.3 | convolution fusion | flops 2214592512 | bytes 9502720 | tf_op jit(solution)/shard_map/dot_general | solution.py:12
  100.9 0.0 copy-done.7
  100.9 6.9 %multiply_convert_fusion.2 = (bf16[384,1408]{1,0:T(8,128)(2,1)S(1)}, bf16[384,1408]{1,0:T(8,128)(2,1)}, bf16[384,1408]{1,0:T(8,128)(2,1)S(1)}) fusion(f32[384,1408]{1,0:T(8,128)S(1)} %fusion, f32[384,1408]{1,0:T(8,128)S(1)} %copy-done.7, bf16[384,2048]{1,0:T(8,128)(2,1)S(1)} %bitcast.74, bf16[1,2048,1408]{2,1,0:T(8,128)(2,1)} %param.10), kind=kOutput, calls=%fused_computation.21 | convolution fusion | flops 2222702592 | bytes 14909440 | tf_op jit(solution)/shard_map/dot_general | solution.py:12
  107.8 0.0 copy-start.5
  107.8 1.0 copy-done.5
  108.8 5.2 %convolution_convert_fusion.2 = bf16[2048,1408]{1,0:T(8,128)(2,1)} fusion(bf16[384,2048]{1,0:T(8,128)(2,1)S(1)} %bitcast.75, bf16[384,1408]{1,0:T(8,128)(2,1)S(1)} %get-tuple-element.12), kind=kOutput, calls=%fused_computation.2 | convolution fusion | flops 2217476096 | bytes 8421376 | tf_op jit(solution)/shard_map/dot_general | solution.py:12
  114.0 0.0 reduce-scatter.4.cloned.1.call-update
  114.0 0.0 reduce-scatter.6.cloned.1.call-start
  114.1 6.5 %convolution_convert_fusion.1 = bf16[2048,1408]{1,0:T(8,128)(2,1)} fusion(bf16[384,2048]{1,0:T(8,128)(2,1)S(1)} %bitcast.76, bf16[384,1408]{1,0:T(8,128)(2,1)} %get-tuple-element.13), kind=kOutput, calls=%fused_computation.1 | convolution fusion | flops 2217476096 | bytes 8421376 | tf_op jit(solution)/shard_map/dot_general | solution.py:12
  120.6 0.0 reduce-scatter.6.cloned.1.call-update
  120.6 0.2 reduce-scatter.8.cloned.1.call-start
  120.8 7.3 %convolution_convert_fusion = bf16[1408,2048]{1,0:T(8,128)(2,1)} fusion(bf16[384,1408]{1,0:T(8,128)(2,1)S(1)} %get-tuple-element.14, bf16[384,2048]{1,0:T(8,128)(2,1)} %bitcast.10), kind=kOutput, calls=%fused_computation | convolution fusion | flops 2217476096 | bytes 8421376 | tf_op jit(solution)/shard_map/dot_general | solution.py:12
  128.1 0.0 reduce-scatter.8.cloned.1.call-update
  128.1 6.4 %fusion.14 = bf16[384,2048]{1,0:T(8,128)(2,1)} fusion(bf16[384,1408]{1,0:T(8,128)(2,1)S(1)} %get-tuple-element.14, bf16[1,1408,2048]{2,1,0:T(8,128)(2,1)} %param.12), kind=kOutput, calls=%fused_computation.17 | convolution fusion | flops 2215378944 | bytes 8421376 | tf_op jit(solution)/shard_map/dot_general | solution.py:12
  134.6 3.7 %all-to-all-start.2 = ((bf16[4,96,2048]{2,1,0:T(8,128)(2,1)}), bf16[4,96,2048]{2,1,0:T(8,128)(2,1)S(1)}, u32[]{:S(2)}, u32[]{:S(2)}) async-start(bf16[4,96,2048]{2,1,0:T(8,128)(2,1)} %bitcast.11), calls=%async_computation.2 | async-start | bytes 3145728 | tf_op jit(solution)/shard_map/all_to_all | solution.py:16
  138.3 0.0 copy-start.6
  138.3 5.1 %fusion.4 = f32[384,2048]{1,0:T(8,128)S(1)} fusion(bf16[384,1408]{1,0:T(8,128)(2,1)} %get-tuple-element.13, bf16[1,2048,1408]{2,1,0:T(8,128)(2,1)} %param.11), kind=kOutput, calls=%fused_computation.7 | convolution fusion | flops 2214592512 | bytes 9994240 | tf_op jit(solution)/shard_map/dot_general | solution.py:12
  143.3 0.0 copy-done.6
  143.3 7.8 %add_convert_fusion = bf16[384,2048]{1,0:T(8,128)(2,1)} fusion(f32[384,2048]{1,0:T(8,128)S(1)} %fusion.4, bf16[384,1408]{1,0:T(8,128)(2,1)S(1)} %copy-done.6, bf16[1,2048,1408]{2,1,0:T(8,128)(2,1)} %param.10), kind=kOutput, calls=%fused_computation.15 | convolution fusion | flops 2216165376 | bytes 11567104 | tf_op jit(solution)/shard_map/dot_general | solution.py:12
  151.2 23.7 %all-to-all-done.2 = bf16[4,96,2048]{2,1,0:T(8,128)(2,1)S(1)} async-done(((bf16[4,96,2048]{2,1,0:T(8,128)(2,1)}), bf16[4,96,2048]{2,1,0:T(8,128)(2,1)S(1)}, u32[]{:S(2)}, u32[]{:S(2)}) %all-to-all-start.2) | async-done | bytes 1572896 | tf_op jit(solution)/shard_map/all_to_all | solution.py:16
  174.9 3.6 %all-to-all-start.3 = ((bf16[4,96,2048]{2,1,0:T(8,128)(2,1)}), bf16[4,96,2048]{2,1,0:T(8,128)(2,1)S(1)}, u32[]{:S(2)}, u32[]{:S(2)}) async-start(bf16[4,96,2048]{2,1,0:T(8,128)(2,1)} %bitcast.77), calls=%async_computation.3 | async-start | bytes 3145728 | tf_op jit(solution)/shard_map/all_to_all | solution.py:16
  178.4 0.0 copy-start.3
  178.4 0.5 fusion.20
  178.9 0.5 copy-done.3
  179.5 1.4 fusion.18
  180.9 0.5 pad_maximum_fusion
  181.4 33.4 %all-to-all-done.3 = bf16[4,96,2048]{2,1,0:T(8,128)(2,1)S(1)} async-done(((bf16[4,96,2048]{2,1,0:T(8,128)(2,1)}), bf16[4,96,2048]{2,1,0:T(8,128)(2,1)S(1)}, u32[]{:S(2)}, u32[]{:S(2)}) %all-to-all-start.3) | async-done | bytes 1572896 | tf_op jit(solution)/shard_map/all_to_all | solution.py:16
  214.8 1.3 convolution_convert_fusion.4
  216.1 0.0 reduce-scatter.4.cloned.1.call-done
  216.1 2.3 bitcast_convert_fusion.2
  218.4 16.8 %reduce-scatter.6.cloned.1.call-done = bf16[256,1408]{1,0:T(8,128)(2,1)} async-done(((bf16[2048,1408]{1,0:T(8,128)(2,1)}), bf16[256,1408]{1,0:T(8,128)(2,1)}) %reduce-scatter.6.cloned.1.call-update) | async-done | bytes 720912 | tf_op jit(solution)/shard_map/reduce_scatter | solution.py:69
  235.3 0.0 copy-start.1
  235.3 2.4 bitcast_convert_fusion.1
  237.6 60.2 %reduce-scatter.8.cloned.1.call-done = bf16[176,2048]{1,0:T(8,128)(2,1)} async-done(((bf16[1408,2048]{1,0:T(8,128)(2,1)}), bf16[176,2048]{1,0:T(8,128)(2,1)}) %reduce-scatter.8.cloned.1.call-update) | async-done | bytes 720912 | tf_op jit(solution)/shard_map/reduce_scatter | solution.py:69
  297.8 2.4 bitcast_convert_fusion
  300.2 0.0 copy-done.1
  (6 shorter events, 0.0 us)
Async XLA Ops:
  7.2 1.7 copy-start
  10.7 6.5 %copy-start.4 = (bf16[128,2]{0,1:T(2,128)(2,1)S(1)}, bf16[128,2]{0,1:T(2,128)(2,1)}, u32[]{:S(2)}) copy-start(bf16[128,2]{0,1:T(2,128)(2,1)} %param.9) | copy-start | bytes 1540
  10.7 6.6 %copy-start.2 = (bf16[128,2048]{1,0:T(8,128)(2,1)S(1)}, bf16[128,2048]{1,0:T(8,128)(2,1)}, u32[]{:S(2)}) copy-start(bf16[128,2048]{1,0:T(8,128)(2,1)} %param.13) | copy-start | bytes 1572868
  10.7 43.4 %all-to-all-start = ((bf16[4,96,2048]{2,1,0:T(8,128)(2,1)}), bf16[4,96,2048]{2,1,0:T(8,128)(2,1)S(1)}, u32[]{:S(2)}, u32[]{:S(2)}) async-start(bf16[4,96,2048]{2,1,0:T(8,128)(2,1)} %bitcast.3), calls=%async_computation | async-start | bytes 3145728 | tf_op jit(solution)/shard_map/all_to_all | solution.py:16
  54.1 40.9 %all-to-all-start.1 = ((bf16[4,96,2048]{2,1,0:T(8,128)(2,1)}), bf16[4,96,2048]{2,1,0:T(8,128)(2,1)}, u32[]{:S(2)}, u32[]{:S(2)}) async-start(bf16[4,96,2048]{2,1,0:T(8,128)(2,1)} %bitcast.9), calls=%async_computation.1 | async-start | bytes 3145728 | tf_op jit(solution)/shard_map/all_to_all | solution.py:16
  58.4 157.7 %reduce-scatter.4.cloned.1.call-start = ((), (), s32[]{:S(2)}) async-start(), calls=%async_computation.7 | async-start | bytes 6488064 | tf_op jit(solution)/shard_map/reduce_scatter | solution.py:69
  95.0 5.9 %copy-start.7 = (f32[384,1408]{1,0:T(8,128)S(1)}, f32[384,1408]{1,0:T(8,128)}, u32[]{:S(2)}) copy-start(f32[384,1408]{1,0:T(8,128)} %fusion.6) | copy-start | bytes 6488068
  107.8 1.0 copy-start.5
  114.0 121.2 %reduce-scatter.6.cloned.1.call-start = ((), (), s32[]{:S(2)}) async-start(), calls=%async_computation.8 | async-start | bytes 6488064 | tf_op jit(solution)/shard_map/reduce_scatter | solution.py:69
  120.6 177.2 %reduce-scatter.8.cloned.1.call-start = ((), (), s32[]{:S(2)}) async-start(), calls=%async_computation.9 | async-start | bytes 6488064 | tf_op jit(solution)/shard_map/reduce_scatter | solution.py:69
  134.6 40.3 %all-to-all-start.2 = ((bf16[4,96,2048]{2,1,0:T(8,128)(2,1)}), bf16[4,96,2048]{2,1,0:T(8,128)(2,1)S(1)}, u32[]{:S(2)}, u32[]{:S(2)}) async-start(bf16[4,96,2048]{2,1,0:T(8,128)(2,1)} %bitcast.11), calls=%async_computation.2 | async-start | bytes 3145728 | tf_op jit(solution)/shard_map/all_to_all | solution.py:16
  138.3 5.1 %copy-start.6 = (bf16[384,1408]{1,0:T(8,128)(2,1)S(1)}, bf16[384,1408]{1,0:T(8,128)(2,1)}, u32[]{:S(2)}) copy-start(bf16[384,1408]{1,0:T(8,128)(2,1)} %copy-done.5) | copy-start | bytes 3244036
  174.9 40.0 %all-to-all-start.3 = ((bf16[4,96,2048]{2,1,0:T(8,128)(2,1)}), bf16[4,96,2048]{2,1,0:T(8,128)(2,1)S(1)}, u32[]{:S(2)}, u32[]{:S(2)}) async-start(bf16[4,96,2048]{2,1,0:T(8,128)(2,1)} %bitcast.77), calls=%async_computation.3 | async-start | bytes 3145728 | tf_op jit(solution)/shard_map/all_to_all | solution.py:16
  178.4 1.0 copy-start.3
  235.3 64.9 %copy-start.1 = (bf16[128,2048]{1,0:T(8,128)(2,1)S(1)}, bf16[128,2048]{1,0:T(8,128)(2,1)}, u32[]{:S(2)}) copy-start(bf16[128,2048]{1,0:T(8,128)(2,1)} %param.7) | copy-start | bytes 1572868
Sparse Core Ops, SparseCore 0:
  114.1 58.1 reduce-scatter.3
  176.2 59.0 reduce-scatter.5
  238.7 59.0 reduce-scatter.7

commit v2 on v1

--- a/solution.py
+++ b/solution.py
@@ -18,6 +18,57 @@
 
 def after(value, *others):
     return lax.optimization_barrier((value, *others))[0]
+
+
+def masks_of(n_rep):
+    masks = []
+    while 1 << len(masks) < n_rep:
+        masks.append(1 << len(masks))
+    return masks
+
+
+def ranked(left):
+    n_rep = lax.axis_size("rep")
+    me = lax.axis_index("rep")
+    block = left.shape[1] // n_rep
+    return [
+        lax.dynamic_slice_in_dim(left, (me ^ j) * block, block, axis=1) for j in range(n_rep)
+    ]
+
+
+class Halving:
+    def __init__(self, blocks, right, order):
+        self.blocks, self.right, self.order = blocks, right, order
+        self.live = [0]
+        for mask in reversed(order):
+            self.live = self.live + [j | mask for j in self.live]
+        self.received = []
+
+    def total(self, low, high):
+        left = jnp.concatenate([self.blocks[j] for j in self.live[low:high]], axis=1)
+        rows = self.blocks[0].shape[1]
+        value = dot(left, self.right, 0, 0)
+        for got in self.received:
+            value = value + got[low * rows : high * rows].astype(F32)
+        return value
+
+    def send(self):
+        stage = len(self.received)
+        n_rep = len(self.live)
+        high = n_rep >> stage
+        part = self.total(high // 2, high).astype(BF16)
+        mask = self.order[stage]
+        self.received.append(lax.ppermute(part, "rep", [(i, i ^ mask) for i in range(n_rep)]))
+        return part
+
+
+def pieces(blocks, right):
+    masks = masks_of(len(blocks))
+    cut = (blocks[0].shape[1] // 2 + 15) // 16 * 16
+    return [
+        Halving([b[:, :cut] for b in blocks], right, masks),
+        Halving([b[:, cut:] for b in blocks], right, masks[:1] + masks[:0:-1]),
+    ]
 
 
 def body(tokens, experts, gates, w_gate, w_up, w_down, cotangent):
@@ -55,30 +106,48 @@
         after(grad_disp, rows_in).reshape(n_experts, capacity, width)
     ).reshape(slots, width)
 
+    rows_ranked = ranked(rows_in)
     gate_pre = dot(rows_in, gate_mat, 1, 0)
     up_pre = dot(rows_in, up_mat, 1, 0)
     sigmoid_g = jax.nn.sigmoid(gate_pre)
     activated = gate_pre * sigmoid_g
+    slope = up_pre * sigmoid_g * (1.0 + gate_pre * (1.0 - sigmoid_g))
     hidden = (activated * up_pre).astype(BF16)
+    hidden, activated, slope = lax.optimization_barrier((hidden, activated, slope))
     expert_out = dot(hidden, down_mat, 1, 0).astype(BF16)
-    returned = exchange(
-        after(expert_out, out_grads).reshape(n_experts, capacity, width)
-    ).reshape(slots, width)
+    hidden_ranked = ranked(hidden)
+    out_grads, expert_out, *hidden_ranked = lax.optimization_barrier(
+        (out_grads, expert_out, *hidden_ranked)
+    )
+    returned = exchange(expert_out.reshape(n_experts, capacity, width)).reshape(slots, width)
 
-    def summed(term):
-        return lax.psum_scatter(term.astype(BF16), "rep", scatter_dimension=0, tiled=True)
-
-    grad_down = summed(dot(hidden, out_grads, 0, 0))
-
-    hidden_grad = dot(out_grads, down_mat, 1, 1)
-    gate_delta = (
-        hidden_grad * up_pre * sigmoid_g * (1.0 + gate_pre * (1.0 - sigmoid_g))
-    ).astype(BF16)
+    down = pieces(hidden_ranked, out_grads)
+    parts = [piece.send() for piece in down]
+    hidden_grad = dot(after(out_grads, *parts), down_mat, 1, 1)
+    gate_delta = (hidden_grad * slope).astype(BF16)
     up_delta = (hidden_grad * activated).astype(BF16)
-    grad_gate = summed(dot(rows_in, gate_delta, 0, 0))
-    grad_up = summed(dot(rows_in, up_delta, 0, 0))
+    gate = pieces(rows_ranked, gate_delta)
+    up = pieces(rows_ranked, up_delta)
+    every = down + gate + up
+    parts = [piece.send() for piece in gate + up]
+    parts += [piece.send() for piece in down]
+    gate_delta, up_delta = lax.optimization_barrier((gate_delta, up_delta, *parts))[:2]
     row_grads = (dot(gate_delta, gate_mat, 1, 1) + dot(up_delta, up_mat, 1, 1)).astype(BF16)
+    for piece in gate + up:
+        piece.send()
+    row_grads, returned, *stage = lax.optimization_barrier(
+        (row_grads, returned, *[piece.received[-1] for piece in every])
+    )
+    for piece, got in zip(every, stage):
+        piece.received[-1] = got
     back_rows = exchange(row_grads.reshape(n_experts, capacity, width)).reshape(slots, width)
+    for piece in every:
+        while len(piece.received) < len(piece.order):
+            piece.send()
+    grad_gate, grad_up, grad_down = (
+        jnp.concatenate([piece.total(0, 1) for piece in pair], axis=0)
+        for pair in (gate, up, down)
+    )
 
     layer_out = 0.0
     dots = []

time: 308 us -> 232 us (0.75)
  waiting for transfers between devices: 199 us -> 89.2 us
  matrix products: 64.7 us -> 83.9 us
  starting transfers between devices: 18.3 us -> 34.5 us
  between operations: 13.9 us -> 1.32 us
  local copies, waits for them, and re-layouts: 1.57 us -> 8.14 us
  other arithmetic: 9.21 us -> 13.5 us
    reduce_scatter x3 -> x0, waiting for transfers between devices: 77 us -> none  [summed(): lax.psum_scatter(term.astype(BF16), 'rep', scatter_dimension=0, tiled=True)]
    all_to_all x4, waiting for transfers between devices: 122 us -> 51.4 us  [exchange(): return lax.all_to_all(rows, 'ep', split_axis=0, concat_axis=0, tiled=True)]
    ppermute x0 -> x18, waiting for transfers between devices: none -> 37.8 us  [send(): lax.ppermute(part, 'rep', [(i, i ^ mask) for i in range(n_rep)])]
    dot_general x15 -> x36, matrix products: 64.7 us -> 83.9 us  [dot(): return lax.dot_general(lhs, rhs, contract, preferred_element_type=F32)]
    ppermute x0 -> x18, starting transfers between devices: none -> 15.4 us  [send(): lax.ppermute(part, 'rep', [(i, i ^ mask) for i in range(n_rep)])]
    add x0 -> x6, other arithmetic: none -> 7.7 us  [total(): value = value + got[low * rows:high * rows].astype(F32)]
    slice x0 -> x13, local copies, waits for them, and re-layouts: none -> 3.66 us  [the longest x7 2.98 us: pieces(): b[:, cut:]]
  transfers between devices with their start and end apart: 7 -> 22, of which waited for: 6 -> 7; matrix products, arithmetic and copies ran while one was open for 16% -> 33% of each run, Pallas kernels for 0% -> 0%
where the time goes in v2:
time: 232 us; the launch traced here: 231 us
  waiting for transfers between devices  89.2 us (38%)
  matrix products  83.9 us (36%)
  starting transfers between devices  34.5 us (15%)
  other arithmetic  13.5 us (6%)
  local copies, waits for them, and re-layouts  8.14 us (4%)
    dot_general x36, matrix products, dot(): return lax.dot_general(lhs, rhs, contract, preferred_element_type=F32)  83.9 us
    all_to_all x4, waiting for transfers between devices, exchange(): return lax.all_to_all(rows, 'ep', split_axis=0, concat_axis=0, tiled=True)  51.4 us
    ppermute x18, waiting for transfers between devices, send(): lax.ppermute(part, 'rep', [(i, i ^ mask) for i in range(n_rep)])  37.8 us
    all_to_all x4, starting transfers between devices, exchange(): return lax.all_to_all(rows, 'ep', split_axis=0, concat_axis=0, tiled=True)  19.1 us
    ppermute x18, starting transfers between devices, send(): lax.ppermute(part, 'rep', [(i, i ^ mask) for i in range(n_rep)])  15.4 us
    add x6, other arithmetic, total(): value = value + got[low * rows:high * rows].astype(F32)  7.7 us
  transfers between devices with their start and end apart: 22, of which 7 were waited for; matrix products, arithmetic and copies ran while one was open for 33% of the time, Pallas kernels for 0%

profile of v2, /device:TPU:0, one launch (start us, length us, event | category | flops | bytes accessed | tf_op | source)
XLA Modules:
  0.0 230.5 jit_solution(383162385183099089)
XLA Ops:
  2.3 1.9 convolution_convert_fusion.5
  4.2 6.4 %all-to-all-start = ((bf16[4,96,2048]{2,1,0:T(8,128)(2,1)}), bf16[4,96,2048]{2,1,0:T(8,128)(2,1)S(1)}, u32[]{:S(2)}, u32[]{:S(2)}) async-start(bf16[4,96,2048]{2,1,0:T(8,128)(2,1)} %bitcast.108), calls=%async_computation | async-start | bytes 3145728 | tf_op jit(solution)/shard_map/all_to_all | solution.py:16
  10.8 1.9 multiply_convert_fusion
  12.7 34.8 %all-to-all-done = bf16[4,96,2048]{2,1,0:T(8,128)(2,1)S(1)} async-done(((bf16[4,96,2048]{2,1,0:T(8,128)(2,1)}), bf16[4,96,2048]{2,1,0:T(8,128)(2,1)S(1)}, u32[]{:S(2)}, u32[]{:S(2)}) %all-to-all-start) | async-done | bytes 1572896 | tf_op jit(solution)/shard_map/all_to_all | solution.py:16
  47.6 1.2 copy-done.5
  48.8 3.6 %all-to-all-start.1 = ((bf16[4,96,2048]{2,1,0:T(8,128)(2,1)}), bf16[4,96,2048]{2,1,0:T(8,128)(2,1)S(1)}, u32[]{:S(2)}, u32[]{:S(2)}) async-start(bf16[4,96,2048]{2,1,0:T(8,128)(2,1)} %bitcast.107), calls=%async_computation.1 | async-start | bytes 3145728 | tf_op jit(solution)/shard_map/all_to_all | solution.py:16
  52.4 5.8 %fusion.6 = f32[384,1408]{1,0:T(8,128)S(1)} fusion(bf16[384,2048]{1,0:T(8,128)(2,1)} %bitcast.96, bf16[1,2048,1408]{2,1,0:T(8,128)(2,1)} %param.11), kind=kOutput, calls=%fused_computation.6 | convolution fusion | flops 2214592512 | bytes 9502720 | tf_op jit(solution)/shard_map/dot_general | solution.py:12
  58.2 7.6 %add_multiply_fusion = (f32[384,1408]{1,0:T(8,128)}, bf16[384,1408]{1,0:T(8,128)(2,1)S(1)}, f32[384,1408]{1,0:T(8,128)}) fusion(f32[384,1408]{1,0:T(8,128)S(1)} %fusion.6, bf16[384,2048]{1,0:T(8,128)(2,1)S(1)} %bitcast.105, bf16[1,2048,1408]{2,1,0:T(8,128)(2,1)} %param.10), kind=kOutput, calls=%fused_computation.25 | convolution fusion | flops 2220539904 | bytes 14909440 | tf_op jit(solution)/shard_map/dot_general | solution.py:12
  65.8 1.1 constant_dynamic-slice_fusion
  66.9 1.5 constant_dynamic-slice_fusion.12
  68.4 3.7 %fusion.14 = bf16[384,2048]{1,0:T(8,128)(2,1)} fusion(bf16[384,1408]{1,0:T(8,128)(2,1)S(1)} %get-tuple-element.32, bf16[1,1408,2048]{2,1,0:T(8,128)(2,1)S(1)} %bitcast.114), kind=kOutput, calls=%fused_computation.18 | convolution fusion | flops 2215378944 | bytes 8421376 | tf_op jit(solution)/shard_map/dot_general | solution.py:12
  72.2 16.6 %all-to-all-done.1 = bf16[4,96,2048]{2,1,0:T(8,128)(2,1)S(1)} async-done(((bf16[4,96,2048]{2,1,0:T(8,128)(2,1)}), bf16[4,96,2048]{2,1,0:T(8,128)(2,1)S(1)}, u32[]{:S(2)}, u32[]{:S(2)}) %all-to-all-start.1) | async-done | bytes 1572896 | tf_op jit(solution)/shard_map/all_to_all | solution.py:16
  89.3 2.4 %convolution_convert_fusion.4 = bf16[384,2048]{1,0:T(8,128)(2,1)} fusion(bf16[384,2048]{1,0:T(8,128)(2,1)S(1)} %bitcast.87, bf16[384,96]{1,0:T(8,128)(2,1)S(1)} %slice.223, bf16[384,96]{1,0:T(8,128)(2,1)S(1)} %slice.222, bf16[384,96]{1,0:T(8,128)(2,1)S(1)} %slice.221, bf16[384,96]{1,0:T(8,128)(2,1)S(1)} %slice.220), kind=kOutput, calls=%fused_computation.19 | convolution fusion | flops 605945856 | bytes 3440640 | tf_op jit(solution)/shard_map/dot_general | solution.py:12
  94.0 2.7 %multiply_convert_fusion.1 = (bf16[384,1408]{1,0:T(8,128)(2,1)S(1)}, bf16[384,1408]{1,0:T(8,128)(2,1)S(1)}) fusion(f32[384,1408]{1,0:T(8,128)S(1)} %copy-done.32, f32[384,1408]{1,0:T(8,128)S(1)} %copy-done.31, bf16[384,2048]{1,0:T(8,128)(2,1)S(1)} %bitcast.89, bf16[1,1408,2048]{2,1,0:T(8,128)(2,1)S(1)} %bitcast.116), kind=kOutput, calls=%fused_computation.23 | convolution fusion | flops 2216755200 | bytes 13828096 | tf_op jit(solution)/shard_map/dot_general | solution.py:12
  96.7 2.1 convolution_convert_fusion.3
  98.8 2.1 convolution_convert_fusion.1
  100.9 2.1 convolution_convert_fusion.2
  103.0 2.1 convolution_convert_fusion
  105.6 1.3 fusion.68
  107.0 1.4 fusion.62
  108.3 2.2 fusion.100
  111.0 2.2 fusion.88
  113.2 2.2 fusion.86
  115.9 2.2 fusion.98
  120.3 4.6 %all-to-all-start.2 = ((bf16[4,96,2048]{2,1,0:T(8,128)(2,1)}), bf16[4,96,2048]{2,1,0:T(8,128)(2,1)}, u32[]{:S(2)}, u32[]{:S(2)}) async-start(bf16[4,96,2048]{2,1,0:T(8,128)(2,1)} %bitcast.109), calls=%async_computation.2 | async-start | bytes 3145728 | tf_op jit(solution)/shard_map/all_to_all | solution.py:16
  124.9 1.9 add_convert_fusion.6
  126.8 1.6 collective-permute-start.3
  128.4 1.7 add_convert_fusion.5
  130.1 1.6 collective-permute-start.5
  131.7 1.7 add_convert_fusion.4
  133.9 1.7 add_convert_fusion.3
  136.3 1.7 add_convert_fusion.2
  138.0 2.9 %add_convert_fusion.1 = bf16[192,2048]{1,0:T(8,128)(2,1)} fusion(bf16[384,2048]{1,0:T(8,128)(2,1)} %collective-permute-done, bf16[384,2048]{1,0:T(8,128)(2,1)S(1)} %bitcast.93, bf16[384,96]{1,0:T(8,128)(2,1)S(1)} %slice.237, bf16[384,96]{1,0:T(8,128)(2,1)S(1)} %copy-done.18), kind=kOutput, calls=%fused_computation.29 | convolution fusion | flops 303464448 | bytes 3293184 | tf_op jit(solution)/shard_map/dot_general | solution.py:12
  140.8 1.5 collective-permute-start.2
  142.3 4.7 %fusion.4 = f32[384,2048]{1,0:T(8,128)S(1)} fusion(bf16[384,1408]{1,0:T(8,128)(2,1)S(1)} %get-tuple-element.45, bf16[1,2048,1408]{2,1,0:T(8,128)(2,1)} %param.11), kind=kOutput, calls=%fused_computation.4 | convolution fusion | flops 2214592512 | bytes 9994240 | tf_op jit(solution)/shard_map/dot_general | solution.py:12
  147.0 1.6 collective-permute-start.11
  148.6 3.8 %add_convert_fusion = bf16[384,2048]{1,0:T(8,128)(2,1)} fusion(f32[384,2048]{1,0:T(8,128)S(1)} %fusion.4, bf16[384,1408]{1,0:T(8,128)(2,1)S(1)} %copy-done.3, bf16[1,2048,1408]{2,1,0:T(8,128)(2,1)S(1)} %bitcast.118), kind=kOutput, calls=%fused_computation.12 | convolution fusion | flops 2216165376 | bytes 11567104 | tf_op jit(solution)/shard_map/dot_general | solution.py:12
  152.4 7.6 %collective-permute-done.7 = bf16[256,1408]{1,0:T(8,128)(2,1)} collective-permute-done((bf16[256,1408]{1,0:T(8,128)(2,1)S(1)}, bf16[256,1408]{1,0:T(8,128)(2,1)}, u32[]{:S(2)}, u32[]{:S(2)}) %collective-permute-start.7) | collective-permute-done | bytes 720928 | tf_op jit(solution)/shard_map/ppermute | solution.py:61
  160.0 4.7 %collective-permute-done.9 = bf16[256,1408]{1,0:T(8,128)(2,1)} collective-permute-done((bf16[256,1408]{1,0:T(8,128)(2,1)S(1)}, bf16[256,1408]{1,0:T(8,128)(2,1)}, u32[]{:S(2)}, u32[]{:S(2)}) %collective-permute-start.9) | collective-permute-done | bytes 720928 | tf_op jit(solution)/shard_map/ppermute | solution.py:61
  164.7 9.9 %collective-permute-done.11 = bf16[256,1408]{1,0:T(8,128)(2,1)} collective-permute-done((bf16[256,1408]{1,0:T(8,128)(2,1)S(1)}, bf16[256,1408]{1,0:T(8,128)(2,1)}, u32[]{:S(2)}, u32[]{:S(2)}) %collective-permute-start.11) | collective-permute-done | bytes 720928 | tf_op jit(solution)/shard_map/ppermute | solution.py:61
  174.6 5.8 %collective-permute-done.2 = bf16[192,2048]{1,0:T(8,128)(2,1)} collective-permute-done((bf16[192,2048]{1,0:T(8,128)(2,1)}, bf16[192,2048]{1,0:T(8,128)(2,1)}, u32[]{:S(2)}, u32[]{:S(2)}) %collective-permute-start.2) | collective-permute-done | bytes 786464 | tf_op jit(solution)/shard_map/ppermute | solution.py:61
  180.4 1.9 fusion.46
  182.3 2.8 %fusion.18 = (bf16[128]{0:T(256)(128)(2,1)S(1)}, bf16[128]{0:T(256)(128)(2,1)S(1)}, bf16[128,2048]{1,0:T(8,128)(2,1)}) fusion(bf16[128,2048]{1,0:T(8,128)(2,1)S(1)} %copy-done.13, f32[128,2048]{1,0:T(8,128)S(1)} %fusion.46, f32[128]{0:T(128)S(1)} %get-tuple-element.86, f32[128]{0:T(128)S(1)} %get-tuple-element.87, bf16[384,2048]{1,0:T(8,128)(2,1)} %bitcast.12, ...), kind=kOutput, calls=%fused_computation.41 | convolution fusion | flops 203734784 | bytes 3672064 | tf_op jit(solution)/shard_map/dot_general | solution.py:12
  185.2 4.5 %all-to-all-start.3 = ((bf16[4,96,2048]{2,1,0:T(8,128)(2,1)}), bf16[4,96,2048]{2,1,0:T(8,128)(2,1)}, u32[]{:S(2)}, u32[]{:S(2)}) async-start(bf16[4,96,2048]{2,1,0:T(8,128)(2,1)} %bitcast.110), calls=%async_computation.3 | async-start | bytes 3145728 | tf_op jit(solution)/shard_map/all_to_all | solution.py:16
  189.7 2.0 add_convert_fusion.11
  191.6 1.6 collective-permute-start.13
  193.2 1.6 add_convert_fusion.12
  195.3 1.6 add_convert_fusion.9
  197.5 1.6 add_convert_fusion.10
  199.1 1.6 collective-permute-start.14
  200.6 1.6 add_convert_fusion.13
  202.3 1.6 collective-permute-start.17
  204.3 1.6 add_convert_fusion.8
  205.9 9.7 %collective-permute-done.17 = bf16[80,2048]{1,0:T(8,128)(2,1)S(1)} collective-permute-done((bf16[80,2048]{1,0:T(8,128)(2,1)S(1)}, bf16[80,2048]{1,0:T(8,128)(2,1)S(1)}, u32[]{:S(2)}, u32[]{:S(2)}) %collective-permute-start.17) | collective-permute-done | bytes 327712 | tf_op jit(solution)/shard_map/ppermute | solution.py:61
  216.1 1.2 convert_add_fusion.5
  217.3 1.3 convert_add_fusion.3
  218.7 1.3 convert_add_fusion.4
  220.0 1.3 convert_add_fusion.1
  221.4 1.2 convert_add_fusion.2
  222.6 1.2 maximum_bitcast_fusion
  223.8 1.2 maximum_bitcast_fusion.1
  225.3 1.3 convert_add_fusion
  226.6 1.2 maximum_bitcast_fusion.2
  227.8 2.7 %convolution_convert_fusion.7 = bf16[128,2048]{1,0:T(8,128)(2,1)} fusion(bf16[384,2048]{1,0:T(8,128)(2,1)} %bitcast.14, s32[128]{0:T(128)S(1)} %get-tuple-element.84, s32[128]{0:T(128)S(1)} %get-tuple-element.85), kind=kOutput, calls=%fused_computation.22 | convolution fusion | flops 201981952 | bytes 2098176 | tf_op jit(solution)/shard_map/dot_general | solution.py:12
  (130 shorter events, 12.1 us)
Async XLA Ops:
  0.6 1.7 copy-start
  4.1 6.5 %copy-start.30 = (bf16[128,2]{0,1:T(2,128)(2,1)S(1)}, bf16[128,2]{0,1:T(2,128)(2,1)}, u32[]{:S(2)}) copy-start(bf16[128,2]{0,1:T(2,128)(2,1)} %param.9) | copy-start | bytes 1540
  4.2 6.7 %copy-start.13 = (bf16[128,2048]{1,0:T(8,128)(2,1)S(1)}, bf16[128,2048]{1,0:T(8,128)(2,1)}, u32[]{:S(2)}) copy-start(bf16[128,2048]{1,0:T(8,128)(2,1)} %param.13) | copy-start | bytes 1572868
  4.2 43.4 %all-to-all-start = ((bf16[4,96,2048]{2,1,0:T(8,128)(2,1)}), bf16[4,96,2048]{2,1,0:T(8,128)(2,1)S(1)}, u32[]{:S(2)}, u32[]{:S(2)}) async-start(bf16[4,96,2048]{2,1,0:T(8,128)(2,1)} %bitcast.108), calls=%async_computation | async-start | bytes 3145728 | tf_op jit(solution)/shard_map/all_to_all | solution.py:16
  47.6 1.2 copy-start.5
  48.8 40.0 %all-to-all-start.1 = ((bf16[4,96,2048]{2,1,0:T(8,128)(2,1)}), bf16[4,96,2048]{2,1,0:T(8,128)(2,1)S(1)}, u32[]{:S(2)}, u32[]{:S(2)}) async-start(bf16[4,96,2048]{2,1,0:T(8,128)(2,1)} %bitcast.107), calls=%async_computation.1 | async-start | bytes 3145728 | tf_op jit(solution)/shard_map/all_to_all | solution.py:16
  52.3 5.9 %copy-start.6 = (bf16[4,96,2048]{2,1,0:T(8,128)(2,1)S(1)}, bf16[4,96,2048]{2,1,0:T(8,128)(2,1)}, u32[]{:S(2)}) copy-start(bf16[4,96,2048]{2,1,0:T(8,128)(2,1)} %copy-done.5) | copy-start | bytes 4718596
  52.4 16.1 %slice-start = ((s8[5767168]{0:T(1024)(128)(4,1)}), s8[4194304]{0:T(1024)(128)(4,1)S(1)}, s32[]{:S(2)}) async-start(s8[5767168]{0:T(1024)(128)(4,1)} %bitcast.113), calls=%async_computation.4 | async-start | bytes 8388608
  58.2 10.2 %slice-start.1 = ((s8[5767168]{0:T(1024)(128)(4,1)}), s8[1572864]{0:T(1024)(128)(4,1)S(1)}, s32[]{:S(2)}) async-start(s8[5767168]{0:T(1024)(128)(4,1)} %bitcast.113), calls=%async_computation.5 | async-start | bytes 3145728
  88.9 3.8 %slice-start.2 = ((s8[5767168]{0:T(1024)(128)(4,1)}), s8[4194304]{0:T(1024)(128)(4,1)S(1)}, s32[]{:S(2)}) async-start(s8[5767168]{0:T(1024)(128)(4,1)} %bitcast.115), calls=%async_computation.6 | async-start | bytes 8388608
  89.3 3.4 %slice-start.3 = ((s8[5767168]{0:T(1024)(128)(4,1)}), s8[1572864]{0:T(1024)(128)(4,1)S(1)}, s32[]{:S(2)}) async-start(s8[5767168]{0:T(1024)(128)(4,1)} %bitcast.115), calls=%async_computation.7 | async-start | bytes 3145728
  91.6 1.7 copy-start.31
  91.6 2.4 %copy-start.32 = (f32[384,1408]{1,0:T(8,128)S(1)}, f32[384,1408]{1,0:T(8,128)}, u32[]{:S(2)}) copy-start(f32[384,1408]{1,0:T(8,128)} %get-tuple-element.40) | copy-start | bytes 6488068
  94.0 2.7 %copy-start.26 = (bf16[384,128]{1,0:T(8,128)(2,1)S(1)}, bf16[384,128]{1,0:T(8,128)(2,1)}, u32[]{:S(2)}) copy-start(bf16[384,128]{1,0:T(8,128)(2,1)} %get-tuple-element.67) | copy-start | bytes 294916
  94.0 2.7 %copy-start.27 = (bf16[384,128]{1,0:T(8,128)(2,1)S(1)}, bf16[384,128]{1,0:T(8,128)(2,1)}, u32[]{:S(2)}) copy-start(bf16[384,128]{1,0:T(8,128)(2,1)} %get-tuple-element.68) | copy-start | bytes 294916
  94.0 2.7 %copy-start.28 = (bf16[384,128]{1,0:T(8,128)(2,1)S(1)}, bf16[384,128]{1,0:T(8,128)(2,1)}, u32[]{:S(2)}) copy-start(bf16[384,128]{1,0:T(8,128)(2,1)} %get-tuple-element.69) | copy-start | bytes 294916
  94.0 2.7 %copy-start.29 = (bf16[384,128]{1,0:T(8,128)(2,1)S(1)}, bf16[384,128]{1,0:T(8,128)(2,1)}, u32[]{:S(2)}) copy-start(bf16[384,128]{1,0:T(8,128)(2,1)} %get-tuple-element.70) | copy-start | bytes 294916
  96.7 14.3 %copy-start.2 = (bf16[384,1408]{1,0:T(8,128)(2,1)}, bf16[384,1408]{1,0:T(8,128)(2,1)S(1)}, u32[]{:S(2)}) copy-start(bf16[384,1408]{1,0:T(8,128)(2,1)S(1)} %get-tuple-element.44) | copy-start | bytes 3244036
  98.8 2.1 copy-start.23
  98.8 2.1 copy-start.24
  98.8 2.1 copy-start.25
  105.1 10.2 %collective-permute-start.1 = (bf16[320,2048]{1,0:T(8,128)(2,1)S(1)}, bf16[320,2048]{1,0:T(8,128)(2,1)}, u32[]{:S(2)}, u32[]{:S(2)}) collective-permute-start(bf16[320,2048]{1,0:T(8,128)(2,1)S(1)} %convolution_convert_fusion.6), channel_id=1, source_target_pairs={{0,4},{4,0},{8,12},{12,8},{16,20},{20,16},{24,28},{28,24},{1,5},{5... | collective-permute-start | bytes 3932168 | tf_op jit(solution)/shard_map/ppermute | solution.py:61
  105.1 21.6 %collective-permute-start.4 = (bf16[512,1408]{1,0:T(8,128)(2,1)}, bf16[512,1408]{1,0:T(8,128)(2,1)}, u32[]{:S(2)}, u32[]{:S(2)}) collective-permute-start(bf16[512,1408]{1,0:T(8,128)(2,1)} %convolution_convert_fusion.3), channel_id=1, source_target_pairs={{0,4},{4,0},{8,12},{12,8},{16,20},{20,16},{24,28},{28,24},{1,5},{5... | collective-permute-start | bytes 4325384 | tf_op jit(solution)/shard_map/ppermute | solution.py:61
  108.3 21.8 %collective-permute-start.6 = (bf16[512,1408]{1,0:T(8,128)(2,1)}, bf16[512,1408]{1,0:T(8,128)(2,1)}, u32[]{:S(2)}, u32[]{:S(2)}) collective-permute-start(bf16[512,1408]{1,0:T(8,128)(2,1)} %convolution_convert_fusion.2), channel_id=1, source_target_pairs={{0,4},{4,0},{8,12},{12,8},{16,20},{20,16},{24,28},{28,24},{1,5},{5... | collective-permute-start | bytes 4325384 | tf_op jit(solution)/shard_map/ppermute | solution.py:61
  110.5 22.9 %collective-permute-start.8 = (bf16[512,1408]{1,0:T(8,128)(2,1)}, bf16[512,1408]{1,0:T(8,128)(2,1)}, u32[]{:S(2)}, u32[]{:S(2)}) collective-permute-start(bf16[512,1408]{1,0:T(8,128)(2,1)} %convolution_convert_fusion.1), channel_id=1, source_target_pairs={{0,4},{4,0},{8,12},{12,8},{16,20},{20,16},{24,28},{28,24},{1,5},{5... | collective-permute-start | bytes 4325384 | tf_op jit(solution)/shard_map/ppermute | solution.py:61
  111.0 24.7 %collective-permute-start.10 = (bf16[512,1408]{1,0:T(8,128)(2,1)}, bf16[512,1408]{1,0:T(8,128)(2,1)}, u32[]{:S(2)}, u32[]{:S(2)}) collective-permute-start(bf16[512,1408]{1,0:T(8,128)(2,1)} %convolution_convert_fusion), channel_id=1, source_target_pairs={{0,4},{4,0},{8,12},{12,8},{16,20},{20,16},{24,28},{28,24},{1,5},{5... | collective-permute-start | bytes 4325384 | tf_op jit(solution)/shard_map/ppermute | solution.py:61
  113.2 4.9 %copy-start.15 = (bf16[384,176]{1,0:T(8,128)(2,1)S(1)}, bf16[384,176]{1,0:T(8,128)(2,1)}, u32[]{:S(2)}) copy-start(bf16[384,176]{1,0:T(8,128)(2,1)} %get-tuple-element.42) | copy-start | bytes 405508
  115.4 3.5 %copy-start.16 = (bf16[384,176]{1,0:T(8,128)(2,1)S(1)}, bf16[384,176]{1,0:T(8,128)(2,1)}, u32[]{:S(2)}) copy-start(bf16[384,176]{1,0:T(8,128)(2,1)} %get-tuple-element.41) | copy-start | bytes 405508
  115.4 4.1 %copy-start.14 = (bf16[384,176]{1,0:T(8,128)(2,1)S(1)}, bf16[384,176]{1,0:T(8,128)(2,1)}, u32[]{:S(2)}) copy-start(bf16[384,176]{1,0:T(8,128)(2,1)} %get-tuple-element.43) | copy-start | bytes 405508
  115.4 22.6 %collective-permute-start = (bf16[384,2048]{1,0:T(8,128)(2,1)}, bf16[384,2048]{1,0:T(8,128)(2,1)}, u32[]{:S(2)}, u32[]{:S(2)}) collective-permute-start(bf16[384,2048]{1,0:T(8,128)(2,1)} %convolution_convert_fusion.4), channel_id=1, source_target_pairs={{0,4},{4,0},{8,12},{12,8},{16,20},{20,16},{24,28},{28,24},{1,5},{5... | collective-permute-start | bytes 4718600 | tf_op jit(solution)/shard_map/ppermute | solution.py:61
  120.3 54.4 %all-to-all-start.2 = ((bf16[4,96,2048]{2,1,0:T(8,128)(2,1)}), bf16[4,96,2048]{2,1,0:T(8,128)(2,1)}, u32[]{:S(2)}, u32[]{:S(2)}) async-start(bf16[4,96,2048]{2,1,0:T(8,128)(2,1)} %bitcast.109), calls=%async_computation.2 | async-start | bytes 3145728 | tf_op jit(solution)/shard_map/all_to_all | solution.py:16
  124.8 3.5 %copy-start.3 = (bf16[384,1408]{1,0:T(8,128)(2,1)S(1)}, bf16[384,1408]{1,0:T(8,128)(2,1)}, u32[]{:S(2)}) copy-start(bf16[384,1408]{1,0:T(8,128)(2,1)} %copy-done.2) | copy-start | bytes 3244036
  124.8 3.5 %copy-start.21 = (bf16[384,128]{1,0:T(8,128)(2,1)S(1)}, bf16[384,128]{1,0:T(8,128)(2,1)}, u32[]{:S(2)}) copy-start(bf16[384,128]{1,0:T(8,128)(2,1)} %get-tuple-element.65) | copy-start | bytes 294916
  124.8 3.5 %copy-start.22 = (bf16[384,128]{1,0:T(8,128)(2,1)S(1)}, bf16[384,128]{1,0:T(8,128)(2,1)}, u32[]{:S(2)}) copy-start(bf16[384,128]{1,0:T(8,128)(2,1)} %get-tuple-element.66) | copy-start | bytes 294916
  126.8 4.9 %copy-start.19 = (bf16[384,128]{1,0:T(8,128)(2,1)S(1)}, bf16[384,128]{1,0:T(8,128)(2,1)}, u32[]{:S(2)}) copy-start(bf16[384,128]{1,0:T(8,128)(2,1)} %get-tuple-element.64) | copy-start | bytes 294916
  126.8 4.9 %copy-start.20 = (bf16[384,128]{1,0:T(8,128)(2,1)S(1)}, bf16[384,128]{1,0:T(8,128)(2,1)}, u32[]{:S(2)}) copy-start(bf16[384,128]{1,0:T(8,128)(2,1)} %get-tuple-element.71) | copy-start | bytes 294916
  126.8 20.2 %collective-permute-start.3 = (bf16[160,2048]{1,0:T(8,128)(2,1)S(1)}, bf16[160,2048]{1,0:T(8,128)(2,1)}, u32[]{:S(2)}, u32[]{:S(2)}) collective-permute-start(bf16[160,2048]{1,0:T(8,128)(2,1)S(1)} %add_convert_fusion.6), channel_id=1, source_target_pairs={{0,16},{4,20},{8,24},{12,28},{16,0},{20,4},{24,8},{28,12},{1,17},{... | collective-permute-start | bytes 1966088 | tf_op jit(solution)/shard_map/ppermute | solution.py:61
  130.1 22.3 %collective-permute-start.5 = (bf16[256,1408]{1,0:T(8,128)(2,1)S(1)}, bf16[256,1408]{1,0:T(8,128)(2,1)}, u32[]{:S(2)}, u32[]{:S(2)}) collective-permute-start(bf16[256,1408]{1,0:T(8,128)(2,1)S(1)} %add_convert_fusion.5), channel_id=1, source_target_pairs={{0,8},{4,12},{8,0},{12,4},{16,24},{20,28},{24,16},{28,20},{1,9},{5... | collective-permute-start | bytes 2162696 | tf_op jit(solution)/shard_map/ppermute | solution.py:61
  133.4 26.6 %collective-permute-start.7 = (bf16[256,1408]{1,0:T(8,128)(2,1)S(1)}, bf16[256,1408]{1,0:T(8,128)(2,1)}, u32[]{:S(2)}, u32[]{:S(2)}) collective-permute-start(bf16[256,1408]{1,0:T(8,128)(2,1)S(1)} %add_convert_fusion.4), channel_id=1, source_target_pairs={{0,16},{4,20},{8,24},{12,28},{16,0},{20,4},{24,8},{28,12},{1,17},{... | collective-permute-start | bytes 2162696 | tf_op jit(solution)/shard_map/ppermute | solution.py:61
  135.6 2.3 %copy-start.18 = (bf16[384,96]{1,0:T(8,128)(2,1)S(1)}, bf16[384,96]{1,0:T(8,128)(2,1)}, u32[]{:S(2)}) copy-start(bf16[384,96]{1,0:T(8,128)(2,1)} %slice.236) | copy-start | bytes 221188
  135.7 29.1 %collective-permute-start.9 = (bf16[256,1408]{1,0:T(8,128)(2,1)S(1)}, bf16[256,1408]{1,0:T(8,128)(2,1)}, u32[]{:S(2)}, u32[]{:S(2)}) collective-permute-start(bf16[256,1408]{1,0:T(8,128)(2,1)S(1)} %add_convert_fusion.3), channel_id=1, source_target_pairs={{0,8},{4,12},{8,0},{12,4},{16,24},{20,28},{24,16},{28,20},{1,9},{5... | collective-permute-start | bytes 2162696 | tf_op jit(solution)/shard_map/ppermute | solution.py:61
  138.0 10.6 %slice-start.4 = ((s8[5767168]{0:T(1024)(128)(4,1)}), s8[4194304]{0:T(1024)(128)(4,1)S(1)}, s32[]{:S(2)}) async-start(s8[5767168]{0:T(1024)(128)(4,1)} %bitcast.117), calls=%async_computation.8 | async-start | bytes 8388608
  140.8 7.8 %slice-start.5 = ((s8[5767168]{0:T(1024)(128)(4,1)}), s8[1572864]{0:T(1024)(128)(4,1)S(1)}, s32[]{:S(2)}) async-start(s8[5767168]{0:T(1024)(128)(4,1)} %bitcast.117), calls=%async_computation.9 | async-start | bytes 3145728
  140.8 39.6 %collective-permute-start.2 = (bf16[192,2048]{1,0:T(8,128)(2,1)}, bf16[192,2048]{1,0:T(8,128)(2,1)}, u32[]{:S(2)}, u32[]{:S(2)}) collective-permute-start(bf16[192,2048]{1,0:T(8,128)(2,1)} %add_convert_fusion.1), channel_id=1, source_target_pairs={{0,8},{4,12},{8,0},{12,4},{16,24},{20,28},{24,16},{28,20},{1,9},{5... | collective-permute-start | bytes 2359304 | tf_op jit(solution)/shard_map/ppermute | solution.py:61
  147.0 27.6 %collective-permute-start.11 = (bf16[256,1408]{1,0:T(8,128)(2,1)S(1)}, bf16[256,1408]{1,0:T(8,128)(2,1)}, u32[]{:S(2)}, u32[]{:S(2)}) collective-permute-start(bf16[256,1408]{1,0:T(8,128)(2,1)S(1)} %add_convert_fusion.2), channel_id=1, source_target_pairs={{0,16},{4,20},{8,24},{12,28},{16,0},{20,4},{24,8},{28,12},{1,17},{... | collective-permute-start | bytes 2162696 | tf_op jit(solution)/shard_map/ppermute | solution.py:61
  185.2 42.7 %all-to-all-start.3 = ((bf16[4,96,2048]{2,1,0:T(8,128)(2,1)}), bf16[4,96,2048]{2,1,0:T(8,128)(2,1)}, u32[]{:S(2)}, u32[]{:S(2)}) async-start(bf16[4,96,2048]{2,1,0:T(8,128)(2,1)} %bitcast.110), calls=%async_computation.3 | async-start | bytes 3145728 | tf_op jit(solution)/shard_map/all_to_all | solution.py:16
  189.7 3.5 %copy-start.4 = (bf16[384,1408]{1,0:T(8,128)(2,1)S(1)}, bf16[384,1408]{1,0:T(8,128)(2,1)}, u32[]{:S(2)}) copy-start(bf16[384,1408]{1,0:T(8,128)(2,1)} %copy-done.2) | copy-start | bytes 3244036
  191.6 25.7 %collective-permute-start.13 = (bf16[128,1408]{1,0:T(8,128)(2,1)S(1)}, bf16[128,1408]{1,0:T(8,128)(2,1)S(1)}, u32[]{:S(2)}, u32[]{:S(2)}) collective-permute-start(bf16[128,1408]{1,0:T(8,128)(2,1)S(1)} %add_convert_fusion.11), channel_id=1, source_target_pairs={{0,8},{4,12},{8,0},{12,4},{16,24},{20,28},{24,16},{28,20},{1,9},{5... | collective-permute-start | bytes 1081352 | tf_op jit(solution)/shard_map/ppermute | solution.py:61
  194.8 23.9 %collective-permute-start.12 = (bf16[128,1408]{1,0:T(8,128)(2,1)S(1)}, bf16[128,1408]{1,0:T(8,128)(2,1)S(1)}, u32[]{:S(2)}, u32[]{:S(2)}) collective-permute-start(bf16[128,1408]{1,0:T(8,128)(2,1)S(1)} %add_convert_fusion.12), channel_id=1, source_target_pairs={{0,16},{4,20},{8,24},{12,28},{16,0},{20,4},{24,8},{28,12},{1,17},{... | collective-permute-start | bytes 1081352 | tf_op jit(solution)/shard_map/ppermute | solution.py:61
  196.9 3.8 %copy-start.17 = (bf16[384,176]{1,0:T(8,128)(2,1)S(1)}, bf16[384,176]{1,0:T(8,128)(2,1)}, u32[]{:S(2)}) copy-start(bf16[384,176]{1,0:T(8,128)(2,1)} %get-tuple-element.41) | copy-start | bytes 405508
  196.9 23.1 %collective-permute-start.15 = (bf16[128,1408]{1,0:T(8,128)(2,1)S(1)}, bf16[128,1408]{1,0:T(8,128)(2,1)S(1)}, u32[]{:S(2)}, u32[]{:S(2)}) collective-permute-start(bf16[128,1408]{1,0:T(8,128)(2,1)S(1)} %add_convert_fusion.9), channel_id=1, source_target_pairs={{0,8},{4,12},{8,0},{12,4},{16,24},{20,28},{24,16},{28,20},{1,9},{5... | collective-permute-start | bytes 1081352 | tf_op jit(solution)/shard_map/ppermute | solution.py:61
  199.1 22.3 %collective-permute-start.14 = (bf16[128,1408]{1,0:T(8,128)(2,1)S(1)}, bf16[128,1408]{1,0:T(8,128)(2,1)S(1)}, u32[]{:S(2)}, u32[]{:S(2)}) collective-permute-start(bf16[128,1408]{1,0:T(8,128)(2,1)S(1)} %add_convert_fusion.10), channel_id=1, source_target_pairs={{0,16},{4,20},{8,24},{12,28},{16,0},{20,4},{24,8},{28,12},{1,17},{... | collective-permute-start | bytes 1081352 | tf_op jit(solution)/shard_map/ppermute | solution.py:61
  202.2 13.9 %copy-start.12 = (f32[80,2048]{1,0:T(8,128)S(1)}, f32[80,2048]{1,0:T(8,128)}, u32[]{:S(2)}) copy-start(f32[80,2048]{1,0:T(8,128)} %fusion.62) | copy-start | bytes 1966084
  202.3 13.3 %collective-permute-start.17 = (bf16[80,2048]{1,0:T(8,128)(2,1)S(1)}, bf16[80,2048]{1,0:T(8,128)(2,1)S(1)}, u32[]{:S(2)}, u32[]{:S(2)}) collective-permute-start(bf16[80,2048]{1,0:T(8,128)(2,1)S(1)} %add_convert_fusion.13), channel_id=1, source_target_pairs={{0,8},{4,12},{8,0},{12,4},{16,24},{20,28},{24,16},{28,20},{1,9},{5... | collective-permute-start | bytes 983048 | tf_op jit(solution)/shard_map/ppermute | solution.py:61
  205.9 11.4 %copy-start.11 = (f32[128,1408]{1,0:T(8,128)S(1)}, f32[128,1408]{1,0:T(8,128)}, u32[]{:S(2)}) copy-start(f32[128,1408]{1,0:T(8,128)} %fusion.88) | copy-start | bytes 2162692
  215.6 9.4 %collective-permute-start.16 = (bf16[96,2048]{1,0:T(8,128)(2,1)S(1)}, bf16[96,2048]{1,0:T(8,128)(2,1)S(1)}, u32[]{:S(2)}, u32[]{:S(2)}) collective-permute-start(bf16[96,2048]{1,0:T(8,128)(2,1)S(1)} %add_convert_fusion.8), channel_id=1, source_target_pairs={{0,16},{4,20},{8,24},{12,28},{16,0},{20,4},{24,8},{28,12},{1,17},{... | collective-permute-start | bytes 1179656 | tf_op jit(solution)/shard_map/ppermute | solution.py:61
  217.3 1.4 copy-start.8
  218.7 1.4 copy-start.9
  220.0 1.4 copy-start.10
  223.8 1.4 copy-start.7
  226.6 4.0 %copy-start.1 = (bf16[128,2048]{1,0:T(8,128)(2,1)S(1)}, bf16[128,2048]{1,0:T(8,128)(2,1)}, u32[]{:S(2)}) copy-start(bf16[128,2048]{1,0:T(8,128)(2,1)} %param.7) | copy-start | bytes 1572868

commit v3 on v2

--- a/solution.py
+++ b/solution.py
@@ -31,8 +31,13 @@
     n_rep = lax.axis_size("rep")
     me = lax.axis_index("rep")
     block = left.shape[1] // n_rep
+    cut = (block // 2 + 15) // 16 * 16
     return [
-        lax.dynamic_slice_in_dim(left, (me ^ j) * block, block, axis=1) for j in range(n_rep)
+        [
+            lax.dynamic_slice_in_dim(left, (me ^ j) * block + low, high - low, axis=1)
+            for j in range(n_rep)
+        ]
+        for low, high in ((0, cut), (cut, block))
     ]
 
 
@@ -62,13 +67,10 @@
         return part
 
 
-def pieces(blocks, right):
-    masks = masks_of(len(blocks))
-    cut = (blocks[0].shape[1] // 2 + 15) // 16 * 16
-    return [
-        Halving([b[:, :cut] for b in blocks], right, masks),
-        Halving([b[:, cut:] for b in blocks], right, masks[:1] + masks[:0:-1]),
-    ]
+def pieces(ranks, right):
+    masks = masks_of(len(ranks[0]))
+    orders = (masks, masks[:1] + masks[:0:-1])
+    return [Halving(blocks, right, order) for blocks, order in zip(ranks, orders)]
 
 
 def body(tokens, experts, gates, w_gate, w_up, w_down, cotangent):
@@ -116,10 +118,12 @@
     hidden, activated, slope = lax.optimization_barrier((hidden, activated, slope))
     expert_out = dot(hidden, down_mat, 1, 0).astype(BF16)
     hidden_ranked = ranked(hidden)
-    out_grads, expert_out, *hidden_ranked = lax.optimization_barrier(
-        (out_grads, expert_out, *hidden_ranked)
-    )
-    returned = exchange(expert_out.reshape(n_experts, capacity, width)).reshape(slots, width)
+    out_grads, expert_out = lax.optimization_barrier((out_grads, expert_out))
+    half = width // 2
+    early = exchange(expert_out[:, :half].reshape(n_experts, capacity, half)).reshape(slots, half)
+    late = exchange(
+        after(expert_out[:, half:], early).reshape(n_experts, capacity, half)
+    ).reshape(slots, half)
 
     down = pieces(hidden_ranked, out_grads)
     parts = [piece.send() for piece in down]
@@ -130,20 +134,21 @@
     up = pieces(rows_ranked, up_delta)
     every = down + gate + up
     parts = [piece.send() for piece in gate + up]
-    parts += [piece.send() for piece in down]
-    gate_delta, up_delta = lax.optimization_barrier((gate_delta, up_delta, *parts))[:2]
+    gate_delta, up_delta, early = lax.optimization_barrier((gate_delta, up_delta, early, *parts))[:3]
     row_grads = (dot(gate_delta, gate_mat, 1, 1) + dot(up_delta, up_mat, 1, 1)).astype(BF16)
-    for piece in gate + up:
+    for piece in down + gate:
         piece.send()
-    row_grads, returned, *stage = lax.optimization_barrier(
-        (row_grads, returned, *[piece.received[-1] for piece in every])
+    row_grads, late, *stage = lax.optimization_barrier(
+        (row_grads, late, *[piece.received[0] for piece in up])
     )
-    for piece, got in zip(every, stage):
-        piece.received[-1] = got
+    for piece, got in zip(up, stage):
+        piece.received[0] = got
+    returned = jnp.concatenate([early, late], axis=1)
     back_rows = exchange(row_grads.reshape(n_experts, capacity, width)).reshape(slots, width)
     for piece in every:
         while len(piece.received) < len(piece.order):
             piece.send()
+        piece.blocks[0] = after(piece.blocks[0], piece.received[-2])
     grad_gate, grad_up, grad_down = (
         jnp.concatenate([piece.total(0, 1) for piece in pair], axis=0)
         for pair in (gate, up, down)

time: 232 us -> 250 us (1.078)
  matrix products: 83.9 us -> 95.3 us
  waiting for transfers between devices: 89.2 us -> 100 us
  other arithmetic: 13.5 us -> 5.82 us
  starting transfers between devices: 34.5 us -> 37.6 us
    all_to_all x4 -> x5, waiting for transfers between devices: 51.4 us -> 67.8 us  [exchange(): return lax.all_to_all(rows, 'ep', split_axis=0, concat_axis=0, tiled=True)]
    dot_general x36, matrix products: 83.9 us -> 95.3 us  [dot(): return lax.dot_general(lhs, rhs, contract, preferred_element_type=F32)]
    add x6 -> x0, other arithmetic: 7.7 us -> none  [total(): value = value + got[low * rows:high * rows].astype(F32)]
    ppermute x18, waiting for transfers between devices: 37.8 us -> 32.5 us  [send(): lax.ppermute(part, 'rep', [(i, i ^ mask) for i in range(n_rep)])]
    all_to_all x4 -> x5, starting transfers between devices: 19.1 us -> 22.4 us  [exchange(): return lax.all_to_all(rows, 'ep', split_axis=0, concat_axis=0, tiled=True)]
  transfers between devices with their start and end apart: 22 -> 23, of which waited for: 7 -> 11; matrix products, arithmetic and copies ran while one was open for 33% -> 40% of each run, Pallas kernels for 0% -> 0%
where the time goes in v3:
time: 250 us; the launch traced here: 248 us
  waiting for transfers between devices  100 us (40%)
  matrix products  95.3 us (38%)
  starting transfers between devices  37.6 us (15%)
  local copies, waits for them, and re-layouts  7.87 us (3%)
  other arithmetic  5.82 us (2%)
    dot_general x36, matrix products, dot(): return lax.dot_general(lhs, rhs, contract, preferred_element_type=F32)  95.3 us
    all_to_all x5, waiting for transfers between devices, exchange(): return lax.all_to_all(rows, 'ep', split_axis=0, concat_axis=0, tiled=True)  67.8 us
    ppermute x18, waiting for transfers between devices, send(): lax.ppermute(part, 'rep', [(i, i ^ mask) for i in range(n_rep)])  32.5 us
    all_to_all x5, starting transfers between devices, exchange(): return lax.all_to_all(rows, 'ep', split_axis=0, concat_axis=0, tiled=True)  22.4 us
    ppermute x18, starting transfers between devices, send(): lax.ppermute(part, 'rep', [(i, i ^ mask) for i in range(n_rep)])  15.2 us
  transfers between devices with their start and end apart: 23, of which 11 were waited for; matrix products, arithmetic and copies ran while one was open for 40% of the time, Pallas kernels for 0%

profile of v3, /device:TPU:0, one launch (start us, length us, event | category | flops | bytes accessed | tf_op | source)
XLA Modules:
  0.0 248.3 jit_solution(823329568103695654)
XLA Ops:
  2.3 1.9 convolution_convert_fusion.5
  4.2 6.4 %all-to-all-start = ((bf16[4,96,2048]{2,1,0:T(8,128)(2,1)}), bf16[4,96,2048]{2,1,0:T(8,128)(2,1)S(1)}, u32[]{:S(2)}, u32[]{:S(2)}) async-start(bf16[4,96,2048]{2,1,0:T(8,128)(2,1)} %bitcast.112), calls=%async_computation | async-start | bytes 3145728 | tf_op jit(solution)/shard_map/all_to_all | solution.py:16
  11.0 1.9 multiply_convert_fusion
  12.8 34.8 %all-to-all-done = bf16[4,96,2048]{2,1,0:T(8,128)(2,1)S(1)} async-done(((bf16[4,96,2048]{2,1,0:T(8,128)(2,1)}), bf16[4,96,2048]{2,1,0:T(8,128)(2,1)S(1)}, u32[]{:S(2)}, u32[]{:S(2)}) %all-to-all-start) | async-done | bytes 1572896 | tf_op jit(solution)/shard_map/all_to_all | solution.py:16
  47.6 3.6 %all-to-all-start.1 = ((bf16[4,96,2048]{2,1,0:T(8,128)(2,1)}), bf16[4,96,2048]{2,1,0:T(8,128)(2,1)S(1)}, u32[]{:S(2)}, u32[]{:S(2)}) async-start(bf16[4,96,2048]{2,1,0:T(8,128)(2,1)} %bitcast.111), calls=%async_computation.1 | async-start | bytes 3145728 | tf_op jit(solution)/shard_map/all_to_all | solution.py:16
  51.2 5.4 %fusion.6 = f32[384,1408]{1,0:T(8,128)S(1)} fusion(bf16[384,2048]{1,0:T(8,128)(2,1)S(1)} %bitcast.104, bf16[1,2048,1408]{2,1,0:T(8,128)(2,1)} %param.11), kind=kOutput, calls=%fused_computation.6 | convolution fusion | flops 2214592512 | bytes 9502720 | tf_op jit(solution)/shard_map/dot_general | solution.py:12
  56.6 7.5 %add_multiply_fusion = (f32[384,1408]{1,0:T(8,128)}, bf16[384,1408]{1,0:T(8,128)(2,1)S(1)}, f32[384,1408]{1,0:T(8,128)}) fusion(f32[384,1408]{1,0:T(8,128)S(1)} %fusion.6, bf16[384,2048]{1,0:T(8,128)(2,1)S(1)} %bitcast.105, bf16[1,2048,1408]{2,1,0:T(8,128)(2,1)} %param.10), kind=kOutput, calls=%fused_computation.43 | convolution fusion | flops 2220539904 | bytes 14909440 | tf_op jit(solution)/shard_map/dot_general | solution.py:12
  65.2 1.2 constant_dynamic-slice_fusion.1
  66.4 1.2 constant_dynamic-slice_fusion.10
  67.6 2.6 %fusion.14 = bf16[384,2048]{1,0:T(8,128)(2,1)S(1)} fusion(bf16[384,1408]{1,0:T(8,128)(2,1)S(1)} %get-tuple-element.28, bf16[1,1408,2048]{2,1,0:T(8,128)(2,1)S(1)} %bitcast.120), kind=kOutput, calls=%fused_computation.18 | convolution fusion | flops 2215378944 | bytes 8421376 | tf_op jit(solution)/shard_map/dot_general | solution.py:12
  70.2 17.4 %all-to-all-done.1 = bf16[4,96,2048]{2,1,0:T(8,128)(2,1)S(1)} async-done(((bf16[4,96,2048]{2,1,0:T(8,128)(2,1)}), bf16[4,96,2048]{2,1,0:T(8,128)(2,1)S(1)}, u32[]{:S(2)}, u32[]{:S(2)}) %all-to-all-start.1) | async-done | bytes 1572896 | tf_op jit(solution)/shard_map/all_to_all | solution.py:16
  87.6 3.2 %convolution_convert_fusion.4 = bf16[384,2048]{1,0:T(8,128)(2,1)} fusion(bf16[384,2048]{1,0:T(8,128)(2,1)S(1)} %bitcast.95, bf16[384,96]{1,0:T(8,128)(2,1)S(1)} %get-tuple-element.75, bf16[384,96]{1,0:T(8,128)(2,1)S(1)} %get-tuple-element.76, bf16[384,96]{1,0:T(8,128)(2,1)S(1)} %get-tuple-element.77, bf16[384,96]{1,0:T(8,128)(2,1)} %get-tuple-element.78), kind=kOutput, calls=%fused_computation.19 | convolution fusion | flops 605945856 | bytes 3440640 | tf_op jit(solution)/shard_map/dot_general | solution.py:12
  90.8 2.1 convolution_convert_fusion.6
  93.4 1.4 fusion.122
  94.8 3.7 %all-to-all-start.2 = ((bf16[4,96,1024]{2,1,0:T(8,128)(2,1)}), bf16[4,96,1024]{2,1,0:T(8,128)(2,1)S(1)}, u32[]{:S(2)}, u32[]{:S(2)}) async-start(bf16[4,96,1024]{2,1,0:T(8,128)(2,1)} %bitcast.11), calls=%async_computation.2 | async-start | bytes 1572864 | tf_op jit(solution)/shard_map/all_to_all | solution.py:16
  98.5 7.5 %multiply_convert_fusion.1 = (bf16[384,1408]{1,0:T(8,128)(2,1)S(1)}, bf16[384,1408]{1,0:T(8,128)(2,1)S(1)}) fusion(f32[384,1408]{1,0:T(8,128)} %get-tuple-element.32, f32[384,1408]{1,0:T(8,128)} %get-tuple-element.31, bf16[384,2048]{1,0:T(8,128)(2,1)S(1)} %bitcast.97, bf16[1,1408,2048]{2,1,0:T(8,128)(2,1)} %param.12), kind=kOutput, calls=%fused_computation.41 | convolution fusion | flops 2216755200 | bytes 13828096 | tf_op jit(solution)/shard_map/dot_general | solution.py:12
  106.1 2.1 convolution_convert_fusion
  108.2 2.1 convolution_convert_fusion.3
  110.8 2.1 convolution_convert_fusion.2
  112.9 2.1 convolution_convert_fusion.1
  115.1 3.8 %all-to-all-done.2 = bf16[4,96,1024]{2,1,0:T(8,128)(2,1)S(1)} async-done(((bf16[4,96,1024]{2,1,0:T(8,128)(2,1)}), bf16[4,96,1024]{2,1,0:T(8,128)(2,1)S(1)}, u32[]{:S(2)}, u32[]{:S(2)}) %all-to-all-start.2) | async-done | bytes 786464 | tf_op jit(solution)/shard_map/all_to_all | solution.py:16
  118.8 7.2 %fusion.4 = f32[384,2048]{1,0:T(8,128)} fusion(bf16[384,1408]{1,0:T(8,128)(2,1)S(1)} %get-tuple-element.36, bf16[1,2048,1408]{2,1,0:T(8,128)(2,1)} %param.11), kind=kOutput, calls=%fused_computation.4 | convolution fusion | flops 2214592512 | bytes 9994240 | tf_op jit(solution)/shard_map/dot_general | solution.py:12
  126.0 3.7 %all-to-all-start.3 = ((bf16[4,96,1024]{2,1,0:T(8,128)(2,1)}), bf16[4,96,1024]{2,1,0:T(8,128)(2,1)S(1)}, u32[]{:S(2)}, u32[]{:S(2)}) async-start(bf16[4,96,1024]{2,1,0:T(8,128)(2,1)} %bitcast.115), calls=%async_computation.3 | async-start | bytes 1572864 | tf_op jit(solution)/shard_map/all_to_all | solution.py:16
  129.7 2.2 constant_dynamic-update-slice_fusion.1
  132.0 8.3 %add_convert_fusion = bf16[384,2048]{1,0:T(8,128)(2,1)} fusion(f32[384,2048]{1,0:T(8,128)} %fusion.4, bf16[384,1408]{1,0:T(8,128)(2,1)S(1)} %copy-done.3, bf16[1,2048,1408]{2,1,0:T(8,128)(2,1)} %param.10), kind=kOutput, calls=%fused_computation.12 | convolution fusion | flops 2216165376 | bytes 11567104 | tf_op jit(solution)/shard_map/dot_general | solution.py:12
  140.3 1.7 add_convert_fusion.6
  142.1 1.6 collective-permute-start.16
  143.7 1.7 add_convert_fusion.5
  145.4 1.6 collective-permute-start.3
  147.0 1.7 add_convert_fusion.3
  149.2 1.8 add_convert_fusion.1
  151.1 8.6 %collective-permute-done.16 = bf16[160,2048]{1,0:T(8,128)(2,1)S(1)} collective-permute-done((bf16[160,2048]{1,0:T(8,128)(2,1)S(1)}, bf16[160,2048]{1,0:T(8,128)(2,1)S(1)}, u32[]{:S(2)}, u32[]{:S(2)}) %collective-permute-start.16) | collective-permute-done | bytes 655392 | tf_op jit(solution)/shard_map/ppermute | solution.py:66
  159.7 1.5 collective-permute-start.13
  161.2 1.6 add_convert_fusion.13
  162.8 1.7 collective-permute-done.3
  164.4 1.5 collective-permute-start.17
  165.9 2.2 add_convert_fusion.12
  168.1 6.6 %collective-permute-done.7 = bf16[256,1408]{1,0:T(8,128)(2,1)S(1)} collective-permute-done((bf16[256,1408]{1,0:T(8,128)(2,1)S(1)}, bf16[256,1408]{1,0:T(8,128)(2,1)S(1)}, u32[]{:S(2)}, u32[]{:S(2)}) %collective-permute-start.7) | collective-permute-done | bytes 720928 | tf_op jit(solution)/shard_map/ppermute | solution.py:66
  174.7 1.5 collective-permute-start.5
  176.2 2.2 add_convert_fusion.11
  178.4 9.1 %collective-permute-done.17 = bf16[80,2048]{1,0:T(8,128)(2,1)S(1)} collective-permute-done((bf16[80,2048]{1,0:T(8,128)(2,1)S(1)}, bf16[80,2048]{1,0:T(8,128)(2,1)S(1)}, u32[]{:S(2)}, u32[]{:S(2)}) %collective-permute-start.17) | collective-permute-done | bytes 327712 | tf_op jit(solution)/shard_map/ppermute | solution.py:66
  187.6 1.5 collective-permute-start.9
  189.1 2.3 fusion.28
  191.4 2.7 %add_convert_fusion.8 = bf16[96,2048]{1,0:T(8,128)(2,1)} fusion(bf16[192,2048]{1,0:T(8,128)(2,1)S(1)} %collective-permute-done.13, bf16[384,2048]{1,0:T(8,128)(2,1)} %collective-permute-done.12, bf16[384,2048]{1,0:T(8,128)(2,1)S(1)} %bitcast.102, bf16[384,1408]{1,0:T(8,128)(2,1)} %copy-done.9, s32[]{:T(128)S(6)} %select_n.123), kind=kOutput, calls=%fused_computation.62 | convolution fusion | flops 151977984 | bytes 2850820 | tf_op jit(solution)/shard_map/dot_general | solution.py:12
  194.6 2.7 %add_convert_fusion.4 = bf16[256,1408]{1,0:T(8,128)(2,1)} fusion(bf16[512,1408]{1,0:T(8,128)(2,1)} %collective-permute-done, bf16[384,1408]{1,0:T(8,128)(2,1)S(1)} %get-tuple-element.36, bf16[384,128]{1,0:T(8,128)(2,1)} %get-tuple-element.60, bf16[384,128]{1,0:T(8,128)(2,1)} %get-tuple-element.56), kind=kOutput, calls=%fused_computation.53 | convolution fusion | flops 278298624 | bytes 2719744 | tf_op jit(solution)/shard_map/dot_general | solution.py:12
  197.8 2.5 %add_convert_fusion.2 = bf16[256,1408]{1,0:T(8,128)(2,1)} fusion(bf16[512,1408]{1,0:T(8,128)(2,1)} %collective-permute-done.1, bf16[384,1408]{1,0:T(8,128)(2,1)S(1)} %get-tuple-element.36, bf16[384,128]{1,0:T(8,128)(2,1)S(1)} %copy-done.25, bf16[384,128]{1,0:T(8,128)(2,1)S(1)} %copy-done.27), kind=kOutput, calls=%fused_computation.51 | convolution fusion | flops 278298624 | bytes 2719744 | tf_op jit(solution)/shard_map/dot_general | solution.py:12
  200.4 1.5 collective-permute-start.8
  203.0 2.0 fusion.30
  205.0 5.0 %all-to-all-start.4 = ((bf16[4,96,2048]{2,1,0:T(8,128)(2,1)}), bf16[4,96,2048]{2,1,0:T(8,128)(2,1)}, u32[]{:S(2)}, u32[]{:S(2)}) async-start(bf16[4,96,2048]{2,1,0:T(8,128)(2,1)} %bitcast.116), calls=%async_computation.4 | async-start | bytes 3145728 | tf_op jit(solution)/shard_map/all_to_all | solution.py:16
  210.5 1.7 fusion.26
  212.3 1.2 maximum_bitcast_fusion.2
  214.5 1.6 add_convert_fusion.10
  216.0 1.6 collective-permute-start.10
  217.6 4.2 %collective-permute-done.8 = bf16[256,1408]{1,0:T(8,128)(2,1)} collective-permute-done((bf16[256,1408]{1,0:T(8,128)(2,1)}, bf16[256,1408]{1,0:T(8,128)(2,1)}, u32[]{:S(2)}, u32[]{:S(2)}) %collective-permute-start.8) | collective-permute-done | bytes 720928 | tf_op jit(solution)/shard_map/ppermute | solution.py:66
  221.9 1.6 add_convert_fusion.9
  223.7 1.5 fusion.24
  225.3 1.5 fusion.22
  226.8 1.2 maximum_bitcast_fusion
  228.0 1.5 fusion.20
  229.6 1.3 collective-permute-done.11
  230.9 1.5 fusion.18
  232.5 1.2 maximum_bitcast_fusion.1
  233.7 11.9 %all-to-all-done.4 = bf16[4,96,2048]{2,1,0:T(8,128)(2,1)} async-done(((bf16[4,96,2048]{2,1,0:T(8,128)(2,1)}), bf16[4,96,2048]{2,1,0:T(8,128)(2,1)}, u32[]{:S(2)}, u32[]{:S(2)}) %all-to-all-start.4) | async-done | bytes 1572896 | tf_op jit(solution)/shard_map/all_to_all | solution.py:16
  245.6 2.7 %convolution_convert_fusion.7 = bf16[128,2048]{1,0:T(8,128)(2,1)} fusion(bf16[384,2048]{1,0:T(8,128)(2,1)} %bitcast.16, s32[128]{0:T(128)S(1)} %get-tuple-element.86, s32[128]{0:T(128)S(1)} %get-tuple-element.87), kind=kOutput, calls=%fused_computation.34 | convolution fusion | flops 201981952 | bytes 2098176 | tf_op jit(solution)/shard_map/dot_general | solution.py:12
  (134 shorter events, 8.7 us)
Async XLA Ops:
  4.2 6.5 %copy-start.45 = (bf16[128,2]{0,1:T(2,128)(2,1)S(1)}, bf16[128,2]{0,1:T(2,128)(2,1)}, u32[]{:S(2)}) copy-start(bf16[128,2]{0,1:T(2,128)(2,1)} %param.9) | copy-start | bytes 1540
  4.2 6.8 %copy-start.10 = (bf16[128,2048]{1,0:T(8,128)(2,1)S(1)}, bf16[128,2048]{1,0:T(8,128)(2,1)}, u32[]{:S(2)}) copy-start(bf16[128,2048]{1,0:T(8,128)(2,1)} %param.13) | copy-start | bytes 1572868
  4.2 43.4 %all-to-all-start = ((bf16[4,96,2048]{2,1,0:T(8,128)(2,1)}), bf16[4,96,2048]{2,1,0:T(8,128)(2,1)S(1)}, u32[]{:S(2)}, u32[]{:S(2)}) async-start(bf16[4,96,2048]{2,1,0:T(8,128)(2,1)} %bitcast.112), calls=%async_computation | async-start | bytes 3145728 | tf_op jit(solution)/shard_map/all_to_all | solution.py:16
  47.6 18.8 %copy-start.6 = (bf16[4,96,2048]{2,1,0:T(8,128)(2,1)}, bf16[4,96,2048]{2,1,0:T(8,128)(2,1)S(1)}, u32[]{:S(2)}) copy-start(bf16[4,96,2048]{2,1,0:T(8,128)(2,1)S(1)} %all-to-all-done) | copy-start | bytes 4718596
  47.6 40.0 %all-to-all-start.1 = ((bf16[4,96,2048]{2,1,0:T(8,128)(2,1)}), bf16[4,96,2048]{2,1,0:T(8,128)(2,1)S(1)}, u32[]{:S(2)}, u32[]{:S(2)}) async-start(bf16[4,96,2048]{2,1,0:T(8,128)(2,1)} %bitcast.111), calls=%async_computation.1 | async-start | bytes 3145728 | tf_op jit(solution)/shard_map/all_to_all | solution.py:16
  51.2 16.5 %slice-start = ((s8[5767168]{0:T(1024)(128)(4,1)}), s8[4194304]{0:T(1024)(128)(4,1)S(1)}, s32[]{:S(2)}) async-start(s8[5767168]{0:T(1024)(128)(4,1)} %bitcast.119), calls=%async_computation.5 | async-start | bytes 8388608
  56.5 11.1 %slice-start.1 = ((s8[5767168]{0:T(1024)(128)(4,1)}), s8[1572864]{0:T(1024)(128)(4,1)S(1)}, s32[]{:S(2)}) async-start(s8[5767168]{0:T(1024)(128)(4,1)} %bitcast.119), calls=%async_computation.6 | async-start | bytes 3145728
  64.1 3.5 %copy-start.9 = (bf16[384,1408]{1,0:T(8,128)(2,1)}, bf16[384,1408]{1,0:T(8,128)(2,1)S(1)}, u32[]{:S(2)}) copy-start(bf16[384,1408]{1,0:T(8,128)(2,1)S(1)} %get-tuple-element.28) | copy-start | bytes 3244036
  87.6 3.2 %copy-start.38 = (bf16[384,80]{1,0:T(8,128)(2,1)S(1)}, bf16[384,80]{1,0:T(8,128)(2,1)}, u32[]{:S(2)}) copy-start(bf16[384,80]{1,0:T(8,128)(2,1)} %get-tuple-element.82) | copy-start | bytes 184324
  87.6 3.2 %copy-start.39 = (bf16[384,80]{1,0:T(8,128)(2,1)S(1)}, bf16[384,80]{1,0:T(8,128)(2,1)}, u32[]{:S(2)}) copy-start(bf16[384,80]{1,0:T(8,128)(2,1)} %get-tuple-element.83) | copy-start | bytes 184324
  87.6 3.2 %copy-start.40 = (bf16[384,80]{1,0:T(8,128)(2,1)S(1)}, bf16[384,80]{1,0:T(8,128)(2,1)}, u32[]{:S(2)}) copy-start(bf16[384,80]{1,0:T(8,128)(2,1)} %get-tuple-element.84) | copy-start | bytes 184324
  87.6 3.2 %copy-start.41 = (bf16[384,80]{1,0:T(8,128)(2,1)S(1)}, bf16[384,80]{1,0:T(8,128)(2,1)}, u32[]{:S(2)}) copy-start(bf16[384,80]{1,0:T(8,128)(2,1)} %get-tuple-element.85) | copy-start | bytes 184324
  90.8 57.9 %collective-permute-start.12 = (bf16[384,2048]{1,0:T(8,128)(2,1)}, bf16[384,2048]{1,0:T(8,128)(2,1)}, u32[]{:S(2)}, u32[]{:S(2)}) collective-permute-start(bf16[384,2048]{1,0:T(8,128)(2,1)} %convolution_convert_fusion.4), channel_id=1, source_target_pairs={{0,4},{4,0},{8,12},{12,8},{16,20},{20,16},{24,28},{28,24},{1,5},{5... | collective-permute-start | bytes 4718600 | tf_op jit(solution)/shard_map/ppermute | solution.py:66
  92.9 47.3 %collective-permute-start.15 = (bf16[320,2048]{1,0:T(8,128)(2,1)}, bf16[320,2048]{1,0:T(8,128)(2,1)}, u32[]{:S(2)}, u32[]{:S(2)}) collective-permute-start(bf16[320,2048]{1,0:T(8,128)(2,1)} %convolution_convert_fusion.6), channel_id=1, source_target_pairs={{0,4},{4,0},{8,12},{12,8},{16,20},{20,16},{24,28},{28,24},{1,5},{5... | collective-permute-start | bytes 3932168 | tf_op jit(solution)/shard_map/ppermute | solution.py:66
  94.8 24.0 %all-to-all-start.2 = ((bf16[4,96,1024]{2,1,0:T(8,128)(2,1)}), bf16[4,96,1024]{2,1,0:T(8,128)(2,1)S(1)}, u32[]{:S(2)}, u32[]{:S(2)}) async-start(bf16[4,96,1024]{2,1,0:T(8,128)(2,1)} %bitcast.11), calls=%async_computation.2 | async-start | bytes 1572864 | tf_op jit(solution)/shard_map/all_to_all | solution.py:16
  98.5 7.5 %copy-start.34 = (bf16[384,128]{1,0:T(8,128)(2,1)S(1)}, bf16[384,128]{1,0:T(8,128)(2,1)}, u32[]{:S(2)}) copy-start(bf16[384,128]{1,0:T(8,128)(2,1)} %get-tuple-element.62) | copy-start | bytes 294916
  98.5 7.5 %copy-start.35 = (bf16[384,128]{1,0:T(8,128)(2,1)S(1)}, bf16[384,128]{1,0:T(8,128)(2,1)}, u32[]{:S(2)}) copy-start(bf16[384,128]{1,0:T(8,128)(2,1)} %get-tuple-element.63) | copy-start | bytes 294916
  98.5 7.5 %copy-start.36 = (bf16[384,128]{1,0:T(8,128)(2,1)S(1)}, bf16[384,128]{1,0:T(8,128)(2,1)}, u32[]{:S(2)}) copy-start(bf16[384,128]{1,0:T(8,128)(2,1)} %get-tuple-element.64) | copy-start | bytes 294916
  98.5 7.5 %copy-start.37 = (bf16[384,128]{1,0:T(8,128)(2,1)S(1)}, bf16[384,128]{1,0:T(8,128)(2,1)}, u32[]{:S(2)}) copy-start(bf16[384,128]{1,0:T(8,128)(2,1)} %get-tuple-element.65) | copy-start | bytes 294916
  106.0 4.8 %copy-start.2 = (bf16[384,1408]{1,0:T(8,128)(2,1)}, bf16[384,1408]{1,0:T(8,128)(2,1)S(1)}, u32[]{:S(2)}) copy-start(bf16[384,1408]{1,0:T(8,128)(2,1)S(1)} %get-tuple-element.35) | copy-start | bytes 3244036
  106.0 2.2 copy-start.30
  108.2 86.3 %collective-permute-start.1 = (bf16[512,1408]{1,0:T(8,128)(2,1)}, bf16[512,1408]{1,0:T(8,128)(2,1)}, u32[]{:S(2)}, u32[]{:S(2)}) collective-permute-start(bf16[512,1408]{1,0:T(8,128)(2,1)} %convolution_convert_fusion), channel_id=1, source_target_pairs={{0,4},{4,0},{8,12},{12,8},{16,20},{20,16},{24,28},{28,24},{1,5},{5... | collective-permute-start | bytes 4325384 | tf_op jit(solution)/shard_map/ppermute | solution.py:66
  110.3 31.7 %collective-permute-start.2 = (bf16[512,1408]{1,0:T(8,128)(2,1)}, bf16[512,1408]{1,0:T(8,128)(2,1)}, u32[]{:S(2)}, u32[]{:S(2)}) collective-permute-start(bf16[512,1408]{1,0:T(8,128)(2,1)} %convolution_convert_fusion.3), channel_id=1, source_target_pairs={{0,4},{4,0},{8,12},{12,8},{16,20},{20,16},{24,28},{28,24},{1,5},{5... | collective-permute-start | bytes 4325384 | tf_op jit(solution)/shard_map/ppermute | solution.py:66
  112.9 32.5 %collective-permute-start.6 = (bf16[512,1408]{1,0:T(8,128)(2,1)}, bf16[512,1408]{1,0:T(8,128)(2,1)}, u32[]{:S(2)}, u32[]{:S(2)}) collective-permute-start(bf16[512,1408]{1,0:T(8,128)(2,1)} %convolution_convert_fusion.2), channel_id=1, source_target_pairs={{0,4},{4,0},{8,12},{12,8},{16,20},{20,16},{24,28},{28,24},{1,5},{5... | collective-permute-start | bytes 4325384 | tf_op jit(solution)/shard_map/ppermute | solution.py:66
  118.8 7.2 %copy-start.7 = (bf16[4,96,1024]{2,1,0:T(8,128)(2,1)}, bf16[4,96,1024]{2,1,0:T(8,128)(2,1)S(1)}, u32[]{:S(2)}) copy-start(bf16[4,96,1024]{2,1,0:T(8,128)(2,1)S(1)} %all-to-all-done.2) | copy-start | bytes 2359300
  126.0 68.5 %all-to-all-start.3 = ((bf16[4,96,1024]{2,1,0:T(8,128)(2,1)}), bf16[4,96,1024]{2,1,0:T(8,128)(2,1)S(1)}, u32[]{:S(2)}, u32[]{:S(2)}) async-start(bf16[4,96,1024]{2,1,0:T(8,128)(2,1)} %bitcast.115), calls=%async_computation.3 | async-start | bytes 1572864 | tf_op jit(solution)/shard_map/all_to_all | solution.py:16
  129.7 2.2 copy-start.3
  131.9 8.3 %copy-start.44 = (bf16[512,1408]{1,0:T(8,128)(2,1)S(1)}, bf16[512,1408]{1,0:T(8,128)(2,1)}, u32[]{:S(2)}) copy-start(bf16[512,1408]{1,0:T(8,128)(2,1)} %convolution_convert_fusion.1) | copy-start | bytes 4325380
  131.9 8.4 %copy-start.22 = (bf16[384,80]{1,0:T(8,128)(2,1)S(1)}, bf16[384,80]{1,0:T(8,128)(2,1)}, u32[]{:S(2)}) copy-start(bf16[384,80]{1,0:T(8,128)(2,1)} %get-tuple-element.79) | copy-start | bytes 184324
  131.9 8.4 %copy-start.23 = (bf16[384,80]{1,0:T(8,128)(2,1)S(1)}, bf16[384,80]{1,0:T(8,128)(2,1)}, u32[]{:S(2)}) copy-start(bf16[384,80]{1,0:T(8,128)(2,1)} %get-tuple-element.80) | copy-start | bytes 184324
  140.2 3.4 %copy-start.28 = (bf16[384,128]{1,0:T(8,128)(2,1)S(1)}, bf16[384,128]{1,0:T(8,128)(2,1)}, u32[]{:S(2)}) copy-start(bf16[384,128]{1,0:T(8,128)(2,1)} %get-tuple-element.56) | copy-start | bytes 294916
  140.2 3.4 %copy-start.29 = (bf16[384,128]{1,0:T(8,128)(2,1)S(1)}, bf16[384,128]{1,0:T(8,128)(2,1)}, u32[]{:S(2)}) copy-start(bf16[384,128]{1,0:T(8,128)(2,1)} %get-tuple-element.60) | copy-start | bytes 294916
  140.2 54.3 %collective-permute-start = (bf16[512,1408]{1,0:T(8,128)(2,1)S(1)}, bf16[512,1408]{1,0:T(8,128)(2,1)}, u32[]{:S(2)}, u32[]{:S(2)}) collective-permute-start(bf16[512,1408]{1,0:T(8,128)(2,1)S(1)} %copy-done.44), channel_id=1, source_target_pairs={{0,4},{4,0},{8,12},{12,8},{16,20},{20,16},{24,28},{28,24},{1,5},{5... | collective-permute-start | bytes 4325384 | tf_op jit(solution)/shard_map/ppermute | solution.py:66
  142.0 4.9 %copy-start.24 = (bf16[384,128]{1,0:T(8,128)(2,1)S(1)}, bf16[384,128]{1,0:T(8,128)(2,1)}, u32[]{:S(2)}) copy-start(bf16[384,128]{1,0:T(8,128)(2,1)} %get-tuple-element.57) | copy-start | bytes 294916
  142.0 4.9 %copy-start.26 = (bf16[384,128]{1,0:T(8,128)(2,1)S(1)}, bf16[384,128]{1,0:T(8,128)(2,1)}, u32[]{:S(2)}) copy-start(bf16[384,128]{1,0:T(8,128)(2,1)} %get-tuple-element.58) | copy-start | bytes 294916
  142.1 17.6 %collective-permute-start.16 = (bf16[160,2048]{1,0:T(8,128)(2,1)S(1)}, bf16[160,2048]{1,0:T(8,128)(2,1)S(1)}, u32[]{:S(2)}, u32[]{:S(2)}) collective-permute-start(bf16[160,2048]{1,0:T(8,128)(2,1)S(1)} %add_convert_fusion.6), channel_id=1, source_target_pairs={{0,16},{4,20},{8,24},{12,28},{16,0},{20,4},{24,8},{28,12},{1,17},{... | collective-permute-start | bytes 1966088 | tf_op jit(solution)/shard_map/ppermute | solution.py:66
  145.4 3.9 %copy-start.20 = (bf16[384,96]{1,0:T(8,128)(2,1)S(1)}, bf16[384,96]{1,0:T(8,128)(2,1)}, u32[]{:S(2)}) copy-start(bf16[384,96]{1,0:T(8,128)(2,1)} %get-tuple-element.72) | copy-start | bytes 221188
  145.4 3.9 %copy-start.21 = (bf16[384,96]{1,0:T(8,128)(2,1)S(1)}, bf16[384,96]{1,0:T(8,128)(2,1)}, u32[]{:S(2)}) copy-start(bf16[384,96]{1,0:T(8,128)(2,1)} %get-tuple-element.73) | copy-start | bytes 221188
  145.4 19.0 %collective-permute-start.3 = (bf16[256,1408]{1,0:T(8,128)(2,1)S(1)}, bf16[256,1408]{1,0:T(8,128)(2,1)S(1)}, u32[]{:S(2)}, u32[]{:S(2)}) collective-permute-start(bf16[256,1408]{1,0:T(8,128)(2,1)S(1)} %add_convert_fusion.5), channel_id=1, source_target_pairs={{0,8},{4,12},{8,0},{12,4},{16,24},{20,28},{24,16},{28,20},{1,9},{5... | collective-permute-start | bytes 2162696 | tf_op jit(solution)/shard_map/ppermute | solution.py:66
  148.7 26.0 %collective-permute-start.7 = (bf16[256,1408]{1,0:T(8,128)(2,1)S(1)}, bf16[256,1408]{1,0:T(8,128)(2,1)S(1)}, u32[]{:S(2)}, u32[]{:S(2)}) collective-permute-start(bf16[256,1408]{1,0:T(8,128)(2,1)S(1)} %add_convert_fusion.3), channel_id=1, source_target_pairs={{0,16},{4,20},{8,24},{12,28},{16,0},{20,4},{24,8},{28,12},{1,17},{... | collective-permute-start | bytes 2162696 | tf_op jit(solution)/shard_map/ppermute | solution.py:66
  159.7 31.7 %collective-permute-start.13 = (bf16[192,2048]{1,0:T(8,128)(2,1)S(1)}, bf16[192,2048]{1,0:T(8,128)(2,1)S(1)}, u32[]{:S(2)}, u32[]{:S(2)}) collective-permute-start(bf16[192,2048]{1,0:T(8,128)(2,1)S(1)} %add_convert_fusion.1), channel_id=1, source_target_pairs={{0,8},{4,12},{8,0},{12,4},{16,24},{20,28},{24,16},{28,20},{1,9},{5... | collective-permute-start | bytes 2359304 | tf_op jit(solution)/shard_map/ppermute | solution.py:66
  164.4 14.0 %copy-start.15 = (bf16[256,1408]{1,0:T(8,128)(2,1)}, bf16[256,1408]{1,0:T(8,128)(2,1)S(1)}, u32[]{:S(2)}) copy-start(bf16[256,1408]{1,0:T(8,128)(2,1)S(1)} %collective-permute-done.3) | copy-start | bytes 2162692
  164.4 23.1 %collective-permute-start.17 = (bf16[80,2048]{1,0:T(8,128)(2,1)S(1)}, bf16[80,2048]{1,0:T(8,128)(2,1)S(1)}, u32[]{:S(2)}, u32[]{:S(2)}) collective-permute-start(bf16[80,2048]{1,0:T(8,128)(2,1)S(1)} %add_convert_fusion.13), channel_id=1, source_target_pairs={{0,8},{4,12},{8,0},{12,4},{16,24},{20,28},{24,16},{28,20},{1,9},{5... | collective-permute-start | bytes 983048 | tf_op jit(solution)/shard_map/ppermute | solution.py:66
  168.1 20.9 %copy-start.19 = (bf16[384,80]{1,0:T(8,128)(2,1)S(1)}, bf16[384,80]{1,0:T(8,128)(2,1)}, u32[]{:S(2)}) copy-start(bf16[384,80]{1,0:T(8,128)(2,1)} %get-tuple-element.47) | copy-start | bytes 184324
  174.7 16.7 %copy-start.17 = (bf16[256,1408]{1,0:T(8,128)(2,1)}, bf16[256,1408]{1,0:T(8,128)(2,1)S(1)}, u32[]{:S(2)}) copy-start(bf16[256,1408]{1,0:T(8,128)(2,1)S(1)} %collective-permute-done.7) | copy-start | bytes 2162692
  174.7 49.0 %collective-permute-start.5 = (bf16[128,1408]{1,0:T(8,128)(2,1)}, bf16[128,1408]{1,0:T(8,128)(2,1)}, u32[]{:S(2)}, u32[]{:S(2)}) collective-permute-start(bf16[128,1408]{1,0:T(8,128)(2,1)} %add_convert_fusion.12), channel_id=1, source_target_pairs={{0,16},{4,20},{8,24},{12,28},{16,0},{20,4},{24,8},{28,12},{1,17},{... | collective-permute-start | bytes 1081352 | tf_op jit(solution)/shard_map/ppermute | solution.py:66
  187.6 37.7 %collective-permute-start.9 = (bf16[128,1408]{1,0:T(8,128)(2,1)}, bf16[128,1408]{1,0:T(8,128)(2,1)}, u32[]{:S(2)}, u32[]{:S(2)}) collective-permute-start(bf16[128,1408]{1,0:T(8,128)(2,1)} %add_convert_fusion.11), channel_id=1, source_target_pairs={{0,8},{4,12},{8,0},{12,4},{16,24},{20,28},{24,16},{28,20},{1,9},{5... | collective-permute-start | bytes 1081352 | tf_op jit(solution)/shard_map/ppermute | solution.py:66
  191.4 3.2 %copy-start.13 = (bf16[192,2048]{1,0:T(8,128)(2,1)}, bf16[192,2048]{1,0:T(8,128)(2,1)S(1)}, u32[]{:S(2)}) copy-start(bf16[192,2048]{1,0:T(8,128)(2,1)S(1)} %collective-permute-done.13) | copy-start | bytes 2359300
  194.0 16.5 %collective-permute-start.14 = (bf16[96,2048]{1,0:T(8,128)(2,1)}, bf16[96,2048]{1,0:T(8,128)(2,1)}, u32[]{:S(2)}, u32[]{:S(2)}) collective-permute-start(bf16[96,2048]{1,0:T(8,128)(2,1)} %add_convert_fusion.8), channel_id=1, source_target_pairs={{0,16},{4,20},{8,24},{12,28},{16,0},{20,4},{24,8},{28,12},{1,17},{... | collective-permute-start | bytes 1179656 | tf_op jit(solution)/shard_map/ppermute | solution.py:66
  194.6 3.3 %copy-start.25 = (bf16[384,128]{1,0:T(8,128)(2,1)S(1)}, bf16[384,128]{1,0:T(8,128)(2,1)}, u32[]{:S(2)}) copy-start(bf16[384,128]{1,0:T(8,128)(2,1)} %get-tuple-element.57) | copy-start | bytes 294916
  194.6 3.3 %copy-start.27 = (bf16[384,128]{1,0:T(8,128)(2,1)S(1)}, bf16[384,128]{1,0:T(8,128)(2,1)}, u32[]{:S(2)}) copy-start(bf16[384,128]{1,0:T(8,128)(2,1)} %get-tuple-element.58) | copy-start | bytes 294916
  197.3 4.6 %copy-start.5 = (bf16[384,2048]{1,0:T(8,128)(2,1)S(1)}, bf16[384,2048]{1,0:T(8,128)(2,1)}, u32[]{:S(2)}) copy-start(bf16[384,2048]{1,0:T(8,128)(2,1)} %constant_dynamic-update-slice_fusion.1) | copy-start | bytes 4718596
  197.3 17.2 %collective-permute-start.4 = (bf16[256,1408]{1,0:T(8,128)(2,1)}, bf16[256,1408]{1,0:T(8,128)(2,1)}, u32[]{:S(2)}, u32[]{:S(2)}) collective-permute-start(bf16[256,1408]{1,0:T(8,128)(2,1)} %add_convert_fusion.4), channel_id=1, source_target_pairs={{0,8},{4,12},{8,0},{12,4},{16,24},{20,28},{24,16},{28,20},{1,9},{5... | collective-permute-start | bytes 2162696 | tf_op jit(solution)/shard_map/ppermute | solution.py:66
  200.4 21.5 %collective-permute-start.8 = (bf16[256,1408]{1,0:T(8,128)(2,1)}, bf16[256,1408]{1,0:T(8,128)(2,1)}, u32[]{:S(2)}, u32[]{:S(2)}) collective-permute-start(bf16[256,1408]{1,0:T(8,128)(2,1)} %add_convert_fusion.2), channel_id=1, source_target_pairs={{0,16},{4,20},{8,24},{12,28},{16,0},{20,4},{24,8},{28,12},{1,17},{... | collective-permute-start | bytes 2162696 | tf_op jit(solution)/shard_map/ppermute | solution.py:66
  205.0 5.0 %copy-start.42 = (bf16[128]{0:T(256)(128)(2,1)S(1)}, bf16[128]{0:T(256)(128)(2,1)}, u32[]{:S(2)}) copy-start(bf16[128]{0:T(256)(128)(2,1)} %get-tuple-element.48) | copy-start | bytes 772
  205.0 5.0 %copy-start.43 = (bf16[128]{0:T(256)(128)(2,1)S(1)}, bf16[128]{0:T(256)(128)(2,1)}, u32[]{:S(2)}) copy-start(bf16[128]{0:T(256)(128)(2,1)} %get-tuple-element.49) | copy-start | bytes 772
  205.0 5.5 %copy-start.14 = (bf16[192,2048]{1,0:T(8,128)(2,1)S(1)}, bf16[192,2048]{1,0:T(8,128)(2,1)}, u32[]{:S(2)}) copy-start(bf16[192,2048]{1,0:T(8,128)(2,1)} %copy-done.13) | copy-start | bytes 2359300
  205.0 40.6 %all-to-all-start.4 = ((bf16[4,96,2048]{2,1,0:T(8,128)(2,1)}), bf16[4,96,2048]{2,1,0:T(8,128)(2,1)}, u32[]{:S(2)}, u32[]{:S(2)}) async-start(bf16[4,96,2048]{2,1,0:T(8,128)(2,1)} %bitcast.116), calls=%async_computation.4 | async-start | bytes 3145728 | tf_op jit(solution)/shard_map/all_to_all | solution.py:16
  216.0 7.7 %copy-start.4 = (bf16[384,1408]{1,0:T(8,128)(2,1)S(1)}, bf16[384,1408]{1,0:T(8,128)(2,1)}, u32[]{:S(2)}) copy-start(bf16[384,1408]{1,0:T(8,128)(2,1)} %copy-done.2) | copy-start | bytes 3244036
  216.0 7.7 %copy-start.12 = (bf16[384,128]{1,0:T(8,128)(2,1)S(1)}, bf16[384,128]{1,0:T(8,128)(2,1)}, u32[]{:S(2)}) copy-start(bf16[384,128]{1,0:T(8,128)(2,1)} %get-tuple-element.42) | copy-start | bytes 294916
  216.0 7.7 %copy-start.16 = (bf16[256,1408]{1,0:T(8,128)(2,1)S(1)}, bf16[256,1408]{1,0:T(8,128)(2,1)}, u32[]{:S(2)}) copy-start(bf16[256,1408]{1,0:T(8,128)(2,1)} %copy-done.15) | copy-start | bytes 2162692
  216.0 12.0 %collective-permute-start.10 = (bf16[128,1408]{1,0:T(8,128)(2,1)S(1)}, bf16[128,1408]{1,0:T(8,128)(2,1)S(1)}, u32[]{:S(2)}, u32[]{:S(2)}) collective-permute-start(bf16[128,1408]{1,0:T(8,128)(2,1)S(1)} %add_convert_fusion.10), channel_id=1, source_target_pairs={{0,16},{4,20},{8,24},{12,28},{16,0},{20,4},{24,8},{28,12},{1,17},{... | collective-permute-start | bytes 1081352 | tf_op jit(solution)/shard_map/ppermute | solution.py:66
  223.4 7.5 %collective-permute-start.11 = (bf16[128,1408]{1,0:T(8,128)(2,1)S(1)}, bf16[128,1408]{1,0:T(8,128)(2,1)S(1)}, u32[]{:S(2)}, u32[]{:S(2)}) collective-permute-start(bf16[128,1408]{1,0:T(8,128)(2,1)S(1)} %add_convert_fusion.9), channel_id=1, source_target_pairs={{0,8},{4,12},{8,0},{12,4},{16,24},{20,28},{24,16},{28,20},{1,9},{5... | collective-permute-start | bytes 1081352 | tf_op jit(solution)/shard_map/ppermute | solution.py:66
  232.5 15.9 %copy-start.1 = (bf16[128,2048]{1,0:T(8,128)(2,1)S(1)}, bf16[128,2048]{1,0:T(8,128)(2,1)}, u32[]{:S(2)}) copy-start(bf16[128,2048]{1,0:T(8,128)(2,1)} %param.7) | copy-start | bytes 1572868
  (7 other events, 12.8 us)
